TPU v7x, 256 devices: a whole 4x4x8 slice. The times are simulated.
256 devices in a mesh: dp: 16 (over x, y_lo, core), seq: 16 (over y_hi, z).
Axes of the slice: x: 4, y: 4 (y_hi: 2, y_lo: 2; y = y_hi * 2 + y_lo), z: 8, core: 2. Of those that a mesh axis runs over, the one named last changes fastest.
Arguments:
- queries: bfloat16 [65536, 32, 128], P(('dp', 'seq')), may hold values from -40 to 40
- keys: bfloat16 [65536, 4, 128], P(('dp', 'seq')), may hold values from -6 to 6
- values: bfloat16 [65536, 4, 128], P(('dp', 'seq')), may hold values from -6 to 6
- upstream: bfloat16 [65536, 32, 128], P(('dp', 'seq')), may hold values from -6 to 6
- rewards: float32 [16, 11], replicated, may hold values from 0 to 4
- response_length: int32 [16, 11], replicated, may hold values from 96 to 1024, as said below
- block_start: int32 [16, 11], replicated, may hold values from 0 to 24, as said below
- move_plan: int32 [16, 11], replicated, may hold values from 0 to 15, as said below
Outputs:
- attn_out: bfloat16 [65536, 32, 128], P(('dp', 'seq'))
- grad_queries: bfloat16 [65536, 32, 128], P(('dp', 'seq'))
- grad_keys: bfloat16 [65536, 4, 128], P(('dp', 'seq'))
- grad_values: bfloat16 [65536, 4, 128], P(('dp', 'seq'))
Inputs may be any that keep to these rules, and one draw needn't show every extreme that they name: `response_length`: rollouts 0 to 7 of a group are short, at most 128 tokens and at least three quarters of that; the others are long, at least 384 tokens. Some short rollout has exactly 128 tokens and some long one exactly 1024 in every draw. `block_start`: short rollout j starts at block j; the long rollouts follow in order, each at the first whole block after the previous one ends. `move_plan`: long rollouts stay in their group. Short rollout j of group g goes to group (g + o_j) mod 16, with 8 distinct offsets o_j: every group receives exactly one short rollout for each slot j and sends at most one to any group.
All inputs are finite; a program needn't handle non-finite values.
Results may differ from a plain program's by a relative error of at most 0.029.
Values may be sent and summed in bfloat16 or wider, within the bound.
A program may use at most 128 MiB of HBM per device.

v0:
```python
import jax
import jax.numpy as jnp
from jax import lax
from jax.sharding import PartitionSpec as P

DH = 128
BLK = 128
LONGS = 3
LW = 1024


def window_scores(query_part, key_part, lengths):
    extent = query_part.shape[1]
    products = jnp.einsum(
        "blcgd,bmcd->bcglm", query_part, key_part, preferred_element_type=jnp.float32
    ) * DH ** (-0.5)
    rows = jnp.arange(extent, dtype=jnp.int32)
    allowed = (rows[None, None, :] <= rows[None, :, None]) & (
        rows[None, :, None] < lengths[:, None, None]
    )
    return (jnp.where(allowed[:, None, None], products, -1e30), allowed)


def forward_pass(query_part, key_part, value_part, lengths):
    scores, allowed = window_scores(query_part, key_part, lengths)
    highest = jnp.max(scores, axis=-1, keepdims=True)
    exponent = jnp.exp(scores - highest)
    row_sum = jnp.sum(exponent, axis=-1, keepdims=True)
    probability = jnp.where(allowed[:, None, None, :, :1], exponent / row_sum, 0.0)
    result = jnp.einsum(
        "bcglm,bmcd->blcgd",
        probability.astype(jnp.bfloat16),
        value_part,
        preferred_element_type=jnp.float32,
    ).astype(jnp.bfloat16)
    return (result, highest, row_sum)


def backward_pass(query_part, key_part, value_part, grad_part, result, highest, row_sum, lengths):
    scores, allowed = window_scores(query_part, key_part, lengths)
    probability = jnp.where(allowed[:, None, None, :, :1], jnp.exp(scores - highest) / row_sum, 0.0)
    prob_half = probability.astype(jnp.bfloat16)
    grad_prob = jnp.einsum(
        "blcgd,bmcd->bcglm", grad_part, value_part, preferred_element_type=jnp.float32
    )
    row_delta = jnp.einsum(
        "blcgd,blcgd->bcgl", grad_part, result, preferred_element_type=jnp.float32
    )
    grad_score = (probability * (grad_prob - row_delta[..., None])).astype(jnp.bfloat16)
    grad_query = (
        jnp.einsum("bcglm,bmcd->blcgd", grad_score, key_part, preferred_element_type=jnp.float32)
        * DH ** (-0.5)
    ).astype(jnp.bfloat16)
    grad_key = jnp.einsum(
        "bcglm,blcgd->bmcd", grad_score, query_part, preferred_element_type=jnp.float32
    ) * DH ** (-0.5)
    grad_value = jnp.einsum(
        "bcglm,blcgd->bmcd", prob_half, grad_part, preferred_element_type=jnp.float32
    )
    return (grad_query, jnp.concatenate([grad_key, grad_value], axis=-1))


def body(queries, keys, values, upstream, rewards, response_length, block_start, move_plan):
    groups = lax.axis_size("dp")
    seq_count = lax.axis_size("seq")
    own_group = lax.axis_index("dp")
    token_rows, heads, head_dim = queries.shape
    kv_count = keys.shape[1]
    shorts = groups // 2
    short_tokens = shorts * BLK
    stacked = jnp.repeat(jnp.concatenate([keys, values], axis=2), seq_count // kv_count, axis=1)
    query_local, pair_local, grad_raw = (
        lax.all_to_all(queries, "seq", split_axis=1, concat_axis=0, tiled=True),
        lax.all_to_all(stacked, "seq", split_axis=1, concat_axis=0, tiled=True),
        lax.all_to_all(upstream, "seq", split_axis=1, concat_axis=0, tiled=True),
    )
    group_tok, local_heads, _ = query_local.shape
    plan_short = move_plan[:, :shorts]
    own_plan = lax.dynamic_index_in_dim(plan_short, own_group, 0, keepdims=False)
    targets = jnp.arange(groups, dtype=jnp.int32)
    send_pick = (own_plan[None, :] == targets[:, None]).astype(jnp.bfloat16)
    short_query = query_local[:short_tokens].reshape(shorts, BLK, local_heads * head_dim)
    short_pair = pair_local[:short_tokens].reshape(shorts, BLK, 2 * head_dim)
    send_query = jnp.einsum(
        "dj,jtf->dtf", send_pick, short_query, preferred_element_type=jnp.float32
    ).astype(jnp.bfloat16)
    send_pair = jnp.einsum(
        "dj,jtf->dtf", send_pick, short_pair, preferred_element_type=jnp.float32
    ).astype(jnp.bfloat16)
    recv_query, recv_pair = (
        lax.all_to_all(send_query, "dp", split_axis=0, concat_axis=0, tiled=True),
        lax.all_to_all(send_pair, "dp", split_axis=0, concat_axis=0, tiled=True),
    )
    arrived = plan_short.T == own_group
    place_pick = arrived.astype(jnp.bfloat16)
    moved_query = jnp.einsum(
        "js,stf->jtf", place_pick, recv_query, preferred_element_type=jnp.float32
    ).astype(jnp.bfloat16)
    moved_pair = jnp.einsum(
        "js,stf->jtf", place_pick, recv_pair, preferred_element_type=jnp.float32
    ).astype(jnp.bfloat16)
    query_bal = jnp.concatenate(
        [moved_query.reshape(short_tokens, local_heads, head_dim), query_local[short_tokens:]],
        axis=0,
    )
    pair_bal = jnp.concatenate(
        [moved_pair.reshape(short_tokens, 1, 2 * head_dim), pair_local[short_tokens:]], axis=0
    )
    source = jnp.sum(jnp.where(arrived, targets[None, :], 0), axis=1)
    short_slots = jnp.arange(shorts, dtype=jnp.int32)
    advantage = rewards - jnp.mean(rewards, axis=1, keepdims=True)
    short_len = response_length[:, :shorts][source, short_slots]
    short_adv = advantage[:, :shorts][source, short_slots]
    own_start = lax.dynamic_index_in_dim(block_start, own_group, 0, keepdims=False)[shorts:] * BLK
    own_len = lax.dynamic_index_in_dim(response_length, own_group, 0, keepdims=False)[shorts:]
    own_adv = lax.dynamic_index_in_dim(advantage, own_group, 0, keepdims=False)[shorts:]
    short_q = query_bal[:short_tokens].reshape(shorts, BLK, 1, local_heads, head_dim)
    short_kv = pair_bal[:short_tokens].reshape(shorts, BLK, 1, 2 * head_dim)
    short_keys = short_kv[..., :head_dim]
    short_values = short_kv[..., head_dim:]
    short_out, short_high, short_sum = forward_pass(short_q, short_keys, short_values, short_len)

    def query_window(offset):
        return lax.dynamic_slice_in_dim(query_bal, offset, LW, 0)[None, :, None]

    def pair_window(offset):
        return lax.dynamic_slice_in_dim(pair_bal, offset, LW, 0)[None]

    def long_forward(bundle):
        offset, length = bundle
        pairs = pair_window(offset)
        result, highest, row_sum = forward_pass(
            query_window(offset), pairs[..., :head_dim], pairs[..., head_dim:], length[None]
        )
        return (result[0], highest[0], row_sum[0])

    long_out, long_high, long_sum = lax.map(long_forward, (own_start, own_len))
    position = jnp.arange(group_tok, dtype=jnp.int32)
    inside = (position[None, :] >= own_start[:, None]) & (
        position[None, :] < own_start[:, None] + own_len[:, None]
    )
    long_weight = jnp.sum(jnp.where(inside, own_adv[:, None], 0.0), axis=0)
    short_weight = jnp.where(
        jnp.arange(BLK, dtype=jnp.int32)[None, :] < short_len[:, None], short_adv[:, None], 0.0
    )
    weight = jnp.concatenate([short_weight.reshape(-1), long_weight[short_tokens:]])
    grad_bal = (weight[:, None, None] * grad_raw.astype(jnp.float32)).astype(jnp.bfloat16)
    short_grad = grad_bal[:short_tokens].reshape(shorts, BLK, 1, local_heads, head_dim)
    short_gq, short_gkv = backward_pass(
        short_q, short_keys, short_values, short_grad, short_out, short_high, short_sum, short_len
    )

    def long_backward(bundle):
        offset, length, result, highest, row_sum = bundle
        pairs = pair_window(offset)
        grad_window = lax.dynamic_slice_in_dim(grad_bal, offset, LW, 0)[None, :, None]
        grad_query, grad_pair = backward_pass(
            query_window(offset),
            pairs[..., :head_dim],
            pairs[..., head_dim:],
            grad_window,
            result[None],
            highest[None],
            row_sum[None],
            length[None],
        )
        return (grad_query[0], grad_pair[0])

    long_gq, long_gkv = lax.map(long_backward, (own_start, own_len, long_out, long_high, long_sum))
    attn_long = jnp.zeros((group_tok, 1, local_heads, head_dim), jnp.bfloat16)
    query_long = jnp.zeros((group_tok, 1, local_heads, head_dim), jnp.bfloat16)
    pair_long = jnp.zeros((group_tok, 1, 2 * head_dim), jnp.float32)
    for number in range(LONGS):
        offset = own_start[number]
        attn_long = lax.dynamic_update_slice_in_dim(
            attn_long,
            lax.dynamic_slice_in_dim(attn_long, offset, LW, 0) + long_out[number],
            offset,
            0,
        )
        query_long = lax.dynamic_update_slice_in_dim(
            query_long,
            lax.dynamic_slice_in_dim(query_long, offset, LW, 0) + long_gq[number],
            offset,
            0,
        )
        pair_long = lax.dynamic_update_slice_in_dim(
            pair_long,
            lax.dynamic_slice_in_dim(pair_long, offset, LW, 0) + long_gkv[number],
            offset,
            0,
        )
    attn_bal = jnp.concatenate(
        [short_out.reshape(short_tokens, 1, local_heads, head_dim), attn_long[short_tokens:]],
        axis=0,
    )
    query_grad_bal = jnp.concatenate(
        [short_gq.reshape(short_tokens, 1, local_heads, head_dim), query_long[short_tokens:]],
        axis=0,
    )
    pair_grad_bal = jnp.concatenate(
        [short_gkv.reshape(short_tokens, 1, 2 * head_dim), pair_long[short_tokens:]], axis=0
    )
    attn_bal = attn_bal.reshape(group_tok, local_heads, head_dim)
    query_grad_bal = query_grad_bal.reshape(group_tok, local_heads, head_dim)
    attn_out, grad_queries = (
        lax.all_to_all(attn_bal, "seq", split_axis=0, concat_axis=1, tiled=True),
        lax.all_to_all(query_grad_bal, "seq", split_axis=0, concat_axis=1, tiled=True),
    )
    sharing = seq_count // kv_count
    key_parts = lax.all_to_all(pair_grad_bal, "seq", split_axis=0, concat_axis=1, tiled=True)
    summed = (
        key_parts.reshape(token_rows, kv_count, sharing, 2 * head_dim)
        .sum(axis=2)
        .astype(jnp.bfloat16)
    )
    return (attn_out, grad_queries, summed[..., :head_dim], summed[..., head_dim:])


def solution(mesh):
    in_specs = (
        P(("dp", "seq"), None, None),
        P(("dp", "seq"), None, None),
        P(("dp", "seq"), None, None),
        P(("dp", "seq"), None, None),
        P(),
        P(),
        P(),
        P(),
    )
    out_specs = (
        P(("dp", "seq"), None, None),
        P(("dp", "seq"), None, None),
        P(("dp", "seq"), None, None),
        P(("dp", "seq"), None, None),
    )
    return jax.shard_map(body, mesh=mesh, in_specs=in_specs, out_specs=out_specs, check_vma=False)
```

profile of v0, /device:TPU:1, one launch (start us, length us, event | category | flops | bytes accessed | tf_op | source)
XLA Modules:
  0.0 646.3 jit_solution(291815685325095053)
XLA Ops:
  3.6 11.7 %all-to-all-start = ((bf16[256,16,256]{2,0,1:T(8,128)(2,1)}), bf16[256,16,256]{2,0,1:T(8,128)(2,1)S(1)}, u32[]{:S(2)}, u32[]{:S(2)}) async-start(bf16[256,16,256]{2,0,1:T(8,128)(2,1)} %bitcast.397), calls=%async_computation | async-start | bytes 4194304 | tf_op jit(solution)/shard_map/all_to_all | solution.py:74
  19.0 45.4 %all-to-all-done = bf16[256,16,256]{2,0,1:T(8,128)(2,1)S(1)} async-done(((bf16[256,16,256]{2,0,1:T(8,128)(2,1)}), bf16[256,16,256]{2,0,1:T(8,128)(2,1)S(1)}, u32[]{:S(2)}, u32[]{:S(2)}) %all-to-all-start) | async-done | bytes 2097184 | tf_op jit(solution)/shard_map/all_to_all | solution.py:74
  64.5 7.2 %all-to-all-start.2 = ((bf16[256,32,128]{2,0,1:T(8,128)(2,1)}), bf16[256,32,128]{2,0,1:T(8,128)(2,1)}, u32[]{:S(2)}, u32[]{:S(2)}) async-start(bf16[256,32,128]{2,0,1:T(8,128)(2,1)} %copy.206), calls=%async_computation.2 | async-start | bytes 4194304 | tf_op jit(solution)/shard_map/all_to_all | solution.py:73
  75.4 45.7 %all-to-all-done.2 = bf16[256,32,128]{2,0,1:T(8,128)(2,1)} async-done(((bf16[256,32,128]{2,0,1:T(8,128)(2,1)}), bf16[256,32,128]{2,0,1:T(8,128)(2,1)}, u32[]{:S(2)}, u32[]{:S(2)}) %all-to-all-start.2) | async-done | bytes 2097184 | tf_op jit(solution)/shard_map/all_to_all | solution.py:73
  121.1 7.0 %all-to-all-start.5 = ((bf16[256,32,128]{2,0,1:T(8,128)(2,1)}), bf16[256,32,128]{2,0,1:T(8,128)(2,1)S(1)}, u32[]{:S(2)}, u32[]{:S(2)}) async-start(bf16[256,32,128]{2,0,1:T(8,128)(2,1)} %copy.225), calls=%async_computation.5 | async-start | bytes 4194304 | tf_op jit(solution)/shard_map/all_to_all | solution.py:75
  141.4 35.9 %all-to-all-done.5 = bf16[256,32,128]{2,0,1:T(8,128)(2,1)S(1)} async-done(((bf16[256,32,128]{2,0,1:T(8,128)(2,1)}), bf16[256,32,128]{2,0,1:T(8,128)(2,1)S(1)}, u32[]{:S(2)}, u32[]{:S(2)}) %all-to-all-start.5) | async-done | bytes 2097184 | tf_op jit(solution)/shard_map/all_to_all | solution.py:75
  177.3 6.2 all-to-all-start.1
  199.2 5.3 all-to-all-start.3
  214.0 6.3 all-to-all-done.3
  235.7 43.0 %while.26 = (s32[]{:T(128)}, bf16[3,1024,1,2,128]{1,4,3,2,0:T(8,128)(2,1)}, f32[3,1,2,1024,1]{3,2,4,1,0:T(2,128)}, f32[3,1,2,1024,1]{3,2,4,1,0:T(2,128)}, s32[3]...) while((s32[]{:T(128)}, ...), condition=%wide.region_6.7_spmd, body=%wide.region_3.6_spmd.sunk | while | flops 1103364096 | bytes 32061620 | solution.py:137
  246.2 3.8 fusion.129
  278.7 4.9 copy.220
  283.6 111.3 %while.27 = (s32[]{:T(128)}, bf16[3,1024,1,2,128]{4,3,1,2,0:T(2,128)(2,1)}, f32[3,1024,1,256]{3,2,1,0:T(1,128)}, s32[3]{0:T(128)S(1)}, bf16[4096,1,256]{2,0,1:T(...) while((s32[]{:T(128)}, ...), condition=%wide.region_10.11_spmd, body=%wide.region_9.10_spmd.sunk | while | flops 2717779968 | bytes 102079784 | solution.py:169
  287.5 5.5 fusion.137
  300.3 6.4 fusion.139
  309.7 4.1 fusion.141
  324.4 5.5 fusion.137
  337.2 6.4 fusion.139
  346.6 4.1 fusion.141
  361.3 5.5 fusion.137
  374.1 6.4 fusion.139
  383.5 4.1 fusion.141
  405.0 19.4 %maximum_bitcast_fusion.1 = bf16[4096,2,128]{2,1,0:T(2,128)(2,1)} fusion(bf16[3072,1,2,128]{3,2,0,1:T(2,128)(2,1)S(1)} %slice.188, bf16[1024,1,2,128]{3,2,0,1:T(2,128)(2,1)S(1)} %copy.236), kind=kLoop, calls=%fused_computation.80 | loop fusion | flops 1048576 | bytes 4194304 | tf_op jit(solution)/shard_map/reshape | solution.py:205
  424.4 6.8 %all-to-all-start.6 = ((bf16[4096,2,128]{2,1,0:T(2,128)(2,1)}), bf16[4096,2,128]{2,1,0:T(2,128)(2,1)}, u32[]{:S(2)}, u32[]{:S(2)}) async-start(bf16[4096,2,128]{2,1,0:T(2,128)(2,1)} %maximum_bitcast_fusion.1), calls=%async_computation.6 | async-start | bytes 4194304 | tf_op jit(solution)/shard_map/all_to_all | solution.py:208
  435.6 19.4 %maximum_bitcast_fusion = bf16[4096,2,128]{2,1,0:T(2,128)(2,1)} fusion(bf16[3072,1,2,128]{3,2,0,1:T(2,128)(2,1)S(1)} %slice.184, bf16[1024,1,2,128]{3,2,0,1:T(2,128)(2,1)S(1)} %copy.223), kind=kLoop, calls=%fused_computation.79 | loop fusion | flops 1048576 | bytes 4194304 | tf_op jit(solution)/shard_map/reshape | solution.py:204
  455.0 24.7 %all-to-all-done.6 = bf16[4096,2,128]{2,1,0:T(2,128)(2,1)} async-done(((bf16[4096,2,128]{2,1,0:T(2,128)(2,1)}), bf16[4096,2,128]{2,1,0:T(2,128)(2,1)}, u32[]{:S(2)}, u32[]{:S(2)}) %all-to-all-start.6) | async-done | bytes 2097184 | tf_op jit(solution)/shard_map/all_to_all | solution.py:208
  479.6 8.0 %all-to-all-start.4 = ((bf16[4096,2,128]{2,1,0:T(2,128)(2,1)}), bf16[4096,2,128]{2,1,0:T(2,128)(2,1)S(1)}, u32[]{:S(2)}, u32[]{:S(2)}) async-start(bf16[4096,2,128]{2,1,0:T(2,128)(2,1)} %maximum_bitcast_fusion), calls=%async_computation.4 | async-start | bytes 4194304 | tf_op jit(solution)/shard_map/all_to_all | solution.py:207
  501.9 22.0 %pad_maximum_fusion.1 = f32[4096,1,256]{2,1,0:T(1,128)} fusion(f32[3072,1,256]{2,1,0:T(1,128)S(1)} %slice.189, f32[1024,1,256]{2,1,0:T(1,128)S(1)} %copy.246), kind=kLoop, calls=%fused_computation.73 | loop fusion | flops 1048576 | bytes 8388608 | tf_op jit(solution)/shard_map/concatenate | solution.py:201
  523.9 13.1 %all-to-all-done.4 = bf16[4096,2,128]{2,1,0:T(2,128)(2,1)S(1)} async-done(((bf16[4096,2,128]{2,1,0:T(2,128)(2,1)}), bf16[4096,2,128]{2,1,0:T(2,128)(2,1)S(1)}, u32[]{:S(2)}, u32[]{:S(2)}) %all-to-all-start.4) | async-done | bytes 2097184 | tf_op jit(solution)/shard_map/all_to_all | solution.py:207
  537.0 7.3 %all-to-all-start.7 = ((f32[4096,1,256]{2,1,0:T(1,128)}), f32[4096,1,256]{2,1,0:T(1,128)}, u32[]{:S(2)}, u32[]{:S(2)}) async-start(f32[4096,1,256]{2,1,0:T(1,128)} %pad_maximum_fusion.1), calls=%async_computation.7 | async-start | bytes 8388608 | tf_op jit(solution)/shard_map/all_to_all | solution.py:211
  544.4 4.3 copy.237
  551.5 89.1 %all-to-all-done.7 = f32[4096,1,256]{2,1,0:T(1,128)} async-done(((f32[4096,1,256]{2,1,0:T(1,128)}), f32[4096,1,256]{2,1,0:T(1,128)}, u32[]{:S(2)}, u32[]{:S(2)}) %all-to-all-start.7) | async-done | bytes 4194336 | tf_op jit(solution)/shard_map/all_to_all | solution.py:211
  (252 shorter events, 185.8 us)
Async XLA Ops:
  0.6 133.1 %copy-start = (s32[16,11]{1,0:T(8,128)S(1)}, s32[16,11]{1,0:T(8,128)}, u32[]{:S(2)}) copy-start(s32[16,11]{1,0:T(8,128)} %param.17) | copy-start | bytes 2116
  3.6 60.9 %all-to-all-start = ((bf16[256,16,256]{2,0,1:T(8,128)(2,1)}), bf16[256,16,256]{2,0,1:T(8,128)(2,1)S(1)}, u32[]{:S(2)}, u32[]{:S(2)}) async-start(bf16[256,16,256]{2,0,1:T(8,128)(2,1)} %bitcast.397), calls=%async_computation | async-start | bytes 4194304 | tf_op jit(solution)/shard_map/all_to_all | solution.py:74
  64.5 10.9 %copy-start.4 = (bf16[256,16,256]{2,0,1:T(8,128)(2,1)}, bf16[256,16,256]{2,0,1:T(8,128)(2,1)S(1)}, u32[]{:S(2)}) copy-start(bf16[256,16,256]{2,0,1:T(8,128)(2,1)S(1)} %all-to-all-done) | copy-start | bytes 6291460
  64.5 56.6 %all-to-all-start.2 = ((bf16[256,32,128]{2,0,1:T(8,128)(2,1)}), bf16[256,32,128]{2,0,1:T(8,128)(2,1)}, u32[]{:S(2)}, u32[]{:S(2)}) async-start(bf16[256,32,128]{2,0,1:T(8,128)(2,1)} %copy.206), calls=%async_computation.2 | async-start | bytes 4194304 | tf_op jit(solution)/shard_map/all_to_all | solution.py:73
  75.4 58.0 %copy-start.22 = (s32[16,11]{1,0:T(8,128)S(1)}, s32[16,11]{1,0:T(8,128)}, u32[]{:S(2)}) copy-start(s32[16,11]{1,0:T(8,128)} %param.19) | copy-start | bytes 2116
  75.4 60.0 %copy-start.21 = (f32[16,11]{1,0:T(8,128)S(1)}, f32[16,11]{1,0:T(8,128)}, u32[]{:S(2)}) copy-start(f32[16,11]{1,0:T(8,128)} %param.16) | copy-start | bytes 2116
  121.1 56.2 %all-to-all-start.5 = ((bf16[256,32,128]{2,0,1:T(8,128)(2,1)}), bf16[256,32,128]{2,0,1:T(8,128)(2,1)S(1)}, u32[]{:S(2)}, u32[]{:S(2)}) async-start(bf16[256,32,128]{2,0,1:T(8,128)(2,1)} %copy.225), calls=%async_computation.5 | async-start | bytes 4194304 | tf_op jit(solution)/shard_map/all_to_all | solution.py:75
  177.3 21.9 %all-to-all-start.1 = ((bf16[16,128,256]{2,1,0:T(8,128)(2,1)}), bf16[16,128,256]{2,1,0:T(8,128)(2,1)S(1)}, u32[]{:S(2)}, u32[]{:S(2)}) async-start(bf16[16,128,256]{2,1,0:T(8,128)(2,1)} %copy.203), calls=%async_computation.1 | async-start | bytes 2097152 | tf_op jit(solution)/shard_map/all_to_all | solution.py:92
  199.2 8.1 %copy-start.11 = (bf16[16,128,256]{2,1,0:T(8,128)(2,1)}, bf16[16,128,256]{2,1,0:T(8,128)(2,1)S(1)}, u32[]{:S(2)}) copy-start(bf16[16,128,256]{2,1,0:T(8,128)(2,1)S(1)} %all-to-all-done.1) | copy-start | bytes 3145732
  199.2 21.0 %all-to-all-start.3 = ((bf16[16,128,256]{2,1,0:T(8,128)(2,1)}), bf16[16,128,256]{2,1,0:T(8,128)(2,1)}, u32[]{:S(2)}, u32[]{:S(2)}) async-start(bf16[16,128,256]{2,1,0:T(8,128)(2,1)} %copy.209), calls=%async_computation.3 | async-start | bytes 2097152 | tf_op jit(solution)/shard_map/all_to_all | solution.py:91
  204.5 2.9 copy-start.7
  207.4 2.8 copy-start.3
  278.7 4.9 copy-start.24
  283.6 111.3 %copy-start.9 = (bf16[8,128,2,128]{1,3,2,0:T(8,128)(2,1)S(1)}, bf16[8,128,2,128]{1,3,2,0:T(8,128)(2,1)}, u32[]{:S(2)}) copy-start(bf16[8,128,2,128]{1,3,2,0:T(8,128)(2,1)} %copy.238) | copy-start | bytes 1572868
  283.6 111.3 %copy-start.14 = (bf16[8,128,128,1]{2,0,1,3:T(8,128)(2,1)S(1)}, bf16[8,128,128,1]{2,0,1,3:T(8,128)(2,1)}, u32[]{:S(2)}) copy-start(bf16[8,128,128,1]{2,0,1,3:T(8,128)(2,1)} %get-tuple-element.229) | copy-start | bytes 786436
  283.6 111.4 %copy-start.20 = (pred[8,128,128]{1,2,0:T(8,128)(4,1)S(1)}, pred[8,128,128]{1,2,0:T(8,128)(4,1)}, u32[]{:S(2)}) copy-start(pred[8,128,128]{1,2,0:T(8,128)(4,1)} %copy.205) | copy-start | bytes 393220
  283.6 111.9 %copy-start.23 = (pred[8,128]{1,0:T(8,128)(4,1)S(1)}, pred[8,128]{1,0:T(8,128)(4,1)}, u32[]{:S(2)}) copy-start(pred[8,128]{1,0:T(8,128)(4,1)} %slice_bitcast_fusion.14) | copy-start | bytes 3076
  299.9 9.8 %slice-start = ((s8[8388608]{0:T(1024)(128)(4,1)}), s8[4194304]{0:T(1024)(128)(4,1)S(1)}, s32[]{:S(2)}) async-start(s8[8388608]{0:T(1024)(128)(4,1)} %bitcast.388), calls=%async_computation.8 | async-start | bytes 8388608 | tf_op jit(solution)/shard_map/while
  300.3 9.4 %slice-start.1 = ((s8[8388608]{0:T(1024)(128)(4,1)}), s8[4194304]{0:T(1024)(128)(4,1)S(1)}, s32[]{:S(2)}) async-start(s8[8388608]{0:T(1024)(128)(4,1)} %bitcast.388), calls=%async_computation.9 | async-start | bytes 8388608 | tf_op jit(solution)/shard_map/while
  306.7 7.2 %copy-start.2 = (bf16[2,1024,1024]{1,2,0:T(8,128)(2,1)}, bf16[2,1024,1024]{1,2,0:T(8,128)(2,1)S(1)}, u32[]{:S(2)}) copy-start(bf16[2,1024,1024]{1,2,0:T(8,128)(2,1)S(1)} %fusion.139) | copy-start | bytes 12582916 | tf_op jit(solution)/shard_map/while
  336.9 9.8 %slice-start = ((s8[8388608]{0:T(1024)(128)(4,1)}), s8[4194304]{0:T(1024)(128)(4,1)S(1)}, s32[]{:S(2)}) async-start(s8[8388608]{0:T(1024)(128)(4,1)} %bitcast.388), calls=%async_computation.8 | async-start | bytes 8388608 | tf_op jit(solution)/shard_map/while
  337.2 9.4 %slice-start.1 = ((s8[8388608]{0:T(1024)(128)(4,1)}), s8[4194304]{0:T(1024)(128)(4,1)S(1)}, s32[]{:S(2)}) async-start(s8[8388608]{0:T(1024)(128)(4,1)} %bitcast.388), calls=%async_computation.9 | async-start | bytes 8388608 | tf_op jit(solution)/shard_map/while
  343.6 7.2 %copy-start.2 = (bf16[2,1024,1024]{1,2,0:T(8,128)(2,1)}, bf16[2,1024,1024]{1,2,0:T(8,128)(2,1)S(1)}, u32[]{:S(2)}) copy-start(bf16[2,1024,1024]{1,2,0:T(8,128)(2,1)S(1)} %fusion.139) | copy-start | bytes 12582916 | tf_op jit(solution)/shard_map/while
  373.8 9.8 %slice-start = ((s8[8388608]{0:T(1024)(128)(4,1)}), s8[4194304]{0:T(1024)(128)(4,1)S(1)}, s32[]{:S(2)}) async-start(s8[8388608]{0:T(1024)(128)(4,1)} %bitcast.388), calls=%async_computation.8 | async-start | bytes 8388608 | tf_op jit(solution)/shard_map/while
  374.1 9.4 %slice-start.1 = ((s8[8388608]{0:T(1024)(128)(4,1)}), s8[4194304]{0:T(1024)(128)(4,1)S(1)}, s32[]{:S(2)}) async-start(s8[8388608]{0:T(1024)(128)(4,1)} %bitcast.388), calls=%async_computation.9 | async-start | bytes 8388608 | tf_op jit(solution)/shard_map/while
  380.5 7.2 %copy-start.2 = (bf16[2,1024,1024]{1,2,0:T(8,128)(2,1)}, bf16[2,1024,1024]{1,2,0:T(8,128)(2,1)S(1)}, u32[]{:S(2)}) copy-start(bf16[2,1024,1024]{1,2,0:T(8,128)(2,1)S(1)} %fusion.139) | copy-start | bytes 12582916 | tf_op jit(solution)/shard_map/while
  398.3 3.3 copy-start.8
  424.4 55.3 %all-to-all-start.6 = ((bf16[4096,2,128]{2,1,0:T(2,128)(2,1)}), bf16[4096,2,128]{2,1,0:T(2,128)(2,1)}, u32[]{:S(2)}, u32[]{:S(2)}) async-start(bf16[4096,2,128]{2,1,0:T(2,128)(2,1)} %maximum_bitcast_fusion.1), calls=%async_computation.6 | async-start | bytes 4194304 | tf_op jit(solution)/shard_map/all_to_all | solution.py:208
  479.6 57.4 %all-to-all-start.4 = ((bf16[4096,2,128]{2,1,0:T(2,128)(2,1)}), bf16[4096,2,128]{2,1,0:T(2,128)(2,1)S(1)}, u32[]{:S(2)}, u32[]{:S(2)}) async-start(bf16[4096,2,128]{2,1,0:T(2,128)(2,1)} %maximum_bitcast_fusion), calls=%async_computation.4 | async-start | bytes 4194304 | tf_op jit(solution)/shard_map/all_to_all | solution.py:207
  491.8 4.7 copy-start.13
  537.0 103.6 %all-to-all-start.7 = ((f32[4096,1,256]{2,1,0:T(1,128)}), f32[4096,1,256]{2,1,0:T(1,128)}, u32[]{:S(2)}, u32[]{:S(2)}) async-start(f32[4096,1,256]{2,1,0:T(1,128)} %pad_maximum_fusion.1), calls=%async_computation.7 | async-start | bytes 8388608 | tf_op jit(solution)/shard_map/all_to_all | solution.py:211
  643.2 2.6 copy-start.1
  (9 other events, 17.6 us)
where the time goes:
time: 656 us; the launch traced here: 646 us
  waiting for transfers between devices  261 us (40%)
  local copies, waits for them, and re-layouts  113 us (17%)
  other arithmetic  96.9 us (15%)
  matrix products  96.9 us (15%)
  starting transfers between devices  59.6 us (9%)
  loops' own time  11.2 us (2%)
  between operations  7.61 us (1%)
    all_to_all x1, waiting for transfers between devices, body(): lax.all_to_all(pair_grad_bal, 'seq', split_axis=0, concat_axis=1, tiled=T...  89.1 us
    all_to_all x1, waiting for transfers between devices, body(): lax.all_to_all(queries, 'seq', split_axis=1, concat_axis=0, tiled=True)  45.7 us
    all_to_all x1, waiting for transfers between devices, body(): lax.all_to_all(stacked, 'seq', split_axis=1, concat_axis=0, tiled=True)  45.4 us
    all_to_all x1, waiting for transfers between devices, body(): lax.all_to_all(upstream, 'seq', split_axis=1, concat_axis=0, tiled=True)  35.9 us
    dot_general x7, matrix products, window_scores(): jnp.einsum('blcgd,bmcd->bcglm', query_part, key_part, preferred_element_t...  25.9 us
    all_to_all x1, waiting for transfers between devices, body(): lax.all_to_all(query_grad_bal, 'seq', split_axis=0, concat_axis=1, tiled=...  24.7 us
    concatenate x1, other arithmetic, body(): jnp.concatenate([short_gkv.reshape(short_tokens, 1, 2 * head_dim), pair_l...  22 us
    dot_general x4, matrix products, backward_pass(): jnp.einsum('blcgd,bmcd->bcglm', grad_part, value_part, preferred_element_...  19.6 us
  transfers between devices with their start and end apart: 8, of which 8 were waited for; matrix products, arithmetic and copies ran while one was open for 16% of the time, Pallas kernels for 0%

commit v1 on v0

v1 whole, which is shorter than its diff:
```python
import functools

import jax
import jax.numpy as jnp
from jax import lax
from jax.experimental import pallas as pl
from jax.experimental.pallas import tpu as pltpu
from jax.sharding import PartitionSpec as P

DH = 128
BLK = 128
LONGS = 3
SHORTS = 8
NEVER = 1 << 20
SCALE = DH**-0.5
EXP_SCALE = SCALE * 1.4426950408889634
NT = (((1,), (1,)), ((), ()))
NN = (((1,), (0,)), ((), ()))


def dot(a, b, dims):
    return lax.dot_general(a, b, dims, preferred_element_type=jnp.float32)


def attend_tile(q, up, start, token, live, weight, load_k, load_v, load_kt, load_vt, add_dk, add_dv, s_ref, p_ref, chunk, chunks, key0):
    rows = q.shape[0]
    highest = jnp.full((1, rows), -1e30, jnp.float32)
    for c in range(chunks):
        s = dot(load_k(c), q, NT)
        key = key0 + c * chunk + lax.broadcasted_iota(jnp.int32, (chunk, rows), 0)
        allowed = key >= start
        if c == chunks - 1:
            allowed = allowed & (key <= token)
        s = jnp.where(allowed, s, -1e30)
        s_ref[c] = s
        highest = jnp.maximum(highest, jnp.max(s, axis=0, keepdims=True))
    shift = highest * EXP_SCALE
    total = jnp.zeros((1, rows), jnp.float32)
    out_t = jnp.zeros((DH, rows), jnp.float32)
    for c in range(chunks):
        p = jnp.exp2(s_ref[c] * EXP_SCALE - shift)
        total = total + jnp.sum(p, axis=0, keepdims=True)
        p16 = p.astype(jnp.bfloat16)
        p_ref[c] = p16
        out_t = out_t + dot(load_vt(c), p16, NN)
    inverse = live / total
    out_t = out_t * inverse
    up_t = up.astype(jnp.float32).T
    scaled = up_t * (weight / total)
    delta = jnp.sum(scaled * out_t, axis=0, keepdims=True)
    scaled16 = scaled.astype(jnp.bfloat16)
    dq_t = jnp.zeros((DH, rows), jnp.float32)
    for c in range(chunks):
        p16 = p_ref[c]
        gp = dot(load_v(c), scaled16, NN)
        ds = (p16.astype(jnp.float32) * (gp - delta)).astype(jnp.bfloat16)
        add_dv(c, dot(p16, scaled16, NT))
        add_dk(c, dot(ds, q, NN))
        dq_t = dq_t + dot(load_kt(c), ds, NN)
    return out_t.T, (dq_t * SCALE).T


def attention_kernel(chunk, q_ref, up_ref, kv_ref, kvt_ref, rows_ref, live_ref, o_ref, dq_ref, dkv_ref, s_ref, p_ref):
    i = pl.program_id(1)
    tiles = pl.num_programs(1)
    tokens = q_ref.shape[0]
    rows = tokens * q_ref.shape[2]
    window = s_ref.shape[0] * chunk
    chunks = s_ref.shape[0]
    b = i // (tiles // 2)

    @pl.when(i == 0)
    def _():
        dkv_ref[...] = jnp.zeros_like(dkv_ref)

    q = q_ref[:, 0].astype(jnp.float32).reshape(rows, DH).astype(jnp.bfloat16)
    up = up_ref[:, 0].astype(jnp.float32).reshape(rows, DH)
    start = rows_ref[0, pl.ds(i, 1), :]
    token = rows_ref[1, pl.ds(i, 1), :]
    live = live_ref[0, pl.ds(i, 1), :]
    weight = live_ref[1, pl.ds(i, 1), :]
    off = pl.multiple_of(b * BLK, BLK)

    def rows_of(c):
        return pl.ds(pl.multiple_of(off + c * chunk, BLK), chunk)

    def add(which):
        def one(c, value):
            dkv_ref[0, which, rows_of(c), :] += value

        return one

    out, dq = attend_tile(
        q, up, start, token, live, weight,
        lambda c: kv_ref[0, 0, rows_of(c), :],
        lambda c: kv_ref[0, 1, rows_of(c), :],
        lambda c: kvt_ref[0, 0, :, rows_of(c)],
        lambda c: kvt_ref[0, 1, :, rows_of(c)],
        add(0), add(1), s_ref, p_ref, chunk, chunks, off,
    )
    o_ref[:, 0] = out.reshape(tokens, -1, DH).astype(jnp.bfloat16)
    dq_ref[:, 0] = dq.reshape(tokens, -1, DH).astype(jnp.bfloat16)

    @pl.when(i == tiles - 1)
    def _():
        dkv_ref[0, 0] = dkv_ref[0, 0] * SCALE


def attention(q, up, kv, rows_i, rows_f):
    tokens, kv_count, per, _ = q.shape
    window = kv.shape[2]
    tile = 256 // per
    tiles = tokens // tile
    chunk = 256
    chunks = (window - BLK) // chunk
    kvt = kv.transpose(0, 1, 3, 2)
    return pl.pallas_call(
        functools.partial(attention_kernel, chunk),
        grid=(kv_count, tiles),
        in_specs=[
            pl.BlockSpec((tile, 1, per, DH), lambda g, i: (i, g, 0, 0)),
            pl.BlockSpec((tile, 1, per, DH), lambda g, i: (i, g, 0, 0)),
            pl.BlockSpec((1, 2, window, DH), lambda g, i: (g, 0, 0, 0)),
            pl.BlockSpec((1, 2, DH, window), lambda g, i: (g, 0, 0, 0)),
            pl.BlockSpec((2, tiles, tile * per), lambda g, i: (0, 0, 0)),
            pl.BlockSpec((2, tiles, tile * per), lambda g, i: (0, 0, 0)),
        ],
        out_specs=[
            pl.BlockSpec((tile, 1, per, DH), lambda g, i: (i, g, 0, 0)),
            pl.BlockSpec((tile, 1, per, DH), lambda g, i: (i, g, 0, 0)),
            pl.BlockSpec((1, 2, window, DH), lambda g, i: (g, 0, 0, 0)),
        ],
        out_shape=[
            jax.ShapeDtypeStruct(q.shape, jnp.bfloat16),
            jax.ShapeDtypeStruct(q.shape, jnp.bfloat16),
            jax.ShapeDtypeStruct(kv.shape, jnp.float32),
        ],
        scratch_shapes=[
            pltpu.VMEM((chunks, chunk, tile * per), jnp.float32),
            pltpu.VMEM((chunks, chunk, tile * per), jnp.bfloat16),
        ],
        compiler_params=pltpu.CompilerParams(vmem_limit_bytes=48 * 1024 * 1024),
    )(q, up, kv, kvt, rows_i, rows_f)


def row_tables(rewards, response_length, block_start, move_plan, own_group, own_seq, tokens, per):
    groups = rewards.shape[0]
    shorts = SHORTS
    advantage = rewards - jnp.mean(rewards, axis=1, keepdims=True)
    arrived = move_plan[:, :shorts] == own_group
    pick = arrived.astype(jnp.float32)
    short_len = jnp.sum(jnp.where(arrived, response_length[:, :shorts], 0), axis=0)
    short_adv = jnp.sum(jnp.where(arrived, advantage[:, :shorts], 0.0), axis=0)
    mine = (jnp.arange(groups) == own_group)[:, None]
    long_start = jnp.sum(jnp.where(mine, block_start[:, shorts:], 0), axis=0) * BLK
    long_len = jnp.sum(jnp.where(mine, response_length[:, shorts:], 0), axis=0)
    long_adv = jnp.sum(jnp.where(mine, advantage[:, shorts:], 0.0), axis=0)
    starts = jnp.concatenate([jnp.arange(shorts, dtype=jnp.int32) * BLK, long_start])
    lens = jnp.concatenate([short_len, long_len])
    advs = jnp.concatenate([short_adv, long_adv])
    position = own_seq * tokens + jnp.arange(tokens, dtype=jnp.int32)
    inside = (position[None, :] >= starts[:, None]) & (position[None, :] < (starts + lens)[:, None])
    live = jnp.any(inside, axis=0)
    start = jnp.sum(jnp.where(inside, starts[:, None], 0), axis=0)
    weight = jnp.sum(jnp.where(inside, advs[:, None], 0.0), axis=0)
    return position, live, start, weight


def shift_pairs(first, last, step):
    if step > 0:
        return [(s, s + 1) for s in range(first, last)]
    return [(s + 1, s) for s in range(first, last)]


def body(queries, keys, values, upstream, rewards, response_length, block_start, move_plan):
    groups = lax.axis_size("dp")
    seq_count = lax.axis_size("seq")
    own_group = lax.axis_index("dp")
    own_seq = lax.axis_index("seq")
    tokens, heads, _ = queries.shape
    kv_count = keys.shape[1]
    per = heads // kv_count
    here = tokens // BLK
    short_rows = SHORTS // here
    piece = BLK // groups

    packed = jnp.concatenate([queries, keys, values], axis=1)
    width = packed.shape[1]
    first = packed.reshape(here, groups, piece, width, DH).transpose(1, 0, 2, 3, 4)
    first = lax.all_to_all(first, "dp", split_axis=0, concat_axis=0, tiled=True)
    slots = jnp.minimum(own_seq * here, SHORTS - here) + jnp.arange(here)
    chosen = jnp.take(move_plan, slots, axis=1)
    every = jnp.arange(groups, dtype=jnp.int32)
    source = jnp.sum(jnp.where(chosen[:, None, :] == every[None, :, None], every[:, None, None], 0), axis=0)
    second = jnp.stack([jnp.take(first[:, n], source[:, n], axis=0) for n in range(here)], axis=1)
    second = lax.all_to_all(second, "dp", split_axis=0, concat_axis=0, tiled=True)
    moved = second.transpose(1, 0, 2, 3, 4).reshape(tokens, width, DH)
    bal = jnp.where(own_seq < short_rows, moved, packed)
    q = bal[:, :heads].reshape(tokens, kv_count, per, DH)
    up = upstream.reshape(tokens, kv_count, per, DH)
    own = bal[:, heads:].reshape(tokens, 2, kv_count, DH).transpose(2, 1, 0, 3)

    ahead = shift_pairs(short_rows, seq_count - 1, 1)
    back = shift_pairs(short_rows, seq_count - 1, -1)
    one = lax.ppermute(own, "seq", ahead)
    two = lax.ppermute(one, "seq", ahead)
    three = lax.ppermute(two, "seq", ahead)
    four = lax.ppermute(three[:, :, BLK:], "seq", ahead)
    window = jnp.concatenate([four, three, two, one, own], axis=2)

    position, live, start, weight = row_tables(
        rewards, response_length, block_start, move_plan, own_group, own_seq, tokens, per
    )
    before = window.shape[2] - tokens
    base = own_seq * tokens - before
    start_w = jnp.where(live, start - base, NEVER)
    token_w = position - base
    tiles = tokens * per // 256
    rows_i = jnp.stack([jnp.repeat(start_w, per), jnp.repeat(token_w, per)]).reshape(2, tiles, 256)
    rows_f = jnp.stack([jnp.repeat(live.astype(jnp.float32), per), jnp.repeat(weight, per)]).reshape(2, tiles, 256)
    out, dq, part = attention(q, up, window, rows_i, rows_f)

    def send(x):
        return lax.ppermute(x.astype(jnp.bfloat16), "seq", back).astype(jnp.float32)

    farthest = send(part[:, :, :BLK])
    a3 = part[:, :, BLK : 3 * BLK] + jnp.pad(farthest, ((0, 0), (0, 0), (BLK, 0), (0, 0)))
    a2 = part[:, :, 3 * BLK : 5 * BLK] + send(a3)
    a1 = part[:, :, 5 * BLK : 7 * BLK] + send(a2)
    a0 = part[:, :, 7 * BLK :] + send(a1)
    grads = a0.astype(jnp.bfloat16).transpose(1, 2, 0, 3)
    return (out.reshape(queries.shape), dq.reshape(queries.shape), grads[0], grads[1])


def solution(mesh):
    spec = P(("dp", "seq"), None, None)
    return jax.shard_map(
        body,
        mesh=mesh,
        in_specs=(spec,) * 4 + (P(),) * 4,
        out_specs=(spec,) * 4,
        check_vma=False,
    )
```

time: 656 us -> 308 us (0.47)
  the two profiles are of different devices: /device:TPU:1 before, /device:TPU:24 now
where the time goes in v1:
time: 308 us; the launch traced here: 307 us
  waiting for transfers between devices  155 us (50%)
  Pallas kernels  55 us (18%)
  starting transfers between devices  43.4 us (14%)
  local copies, waits for them, and re-layouts  41.3 us (13%)
  other arithmetic  11.3 us (4%)
    pallas_call x1, Pallas kernels, attention(): pl.pallas_call(functools.partial(attention_kernel, chunk), grid=(kv_count...  55 us
    all_to_all x1, waiting for transfers between devices, body(): lax.all_to_all(second, 'dp', split_axis=0, concat_axis=0, tiled=True)  35.4 us
    all_to_all x1, waiting for transfers between devices, body(): first = lax.all_to_all(first, 'dp', split_axis=0, concat_axis=0, tiled=True)  35.2 us
    ppermute x4, waiting for transfers between devices, send(): return lax.ppermute(x.astype(jnp.bfloat16), 'seq', back).astype(jnp.float32)  27 us
    ppermute x4, starting transfers between devices, send(): return lax.ppermute(x.astype(jnp.bfloat16), 'seq', back).astype(jnp.float32)  23.5 us
    ppermute x1, waiting for transfers between devices, body(): two = lax.ppermute(one, 'seq', ahead)  16.9 us
    ppermute x1, waiting for transfers between devices, body(): one = lax.ppermute(own, 'seq', ahead)  16.8 us
    ppermute x1, waiting for transfers between devices, body(): three = lax.ppermute(two, 'seq', ahead)  16.1 us
  transfers between devices with their start and end apart: 10, of which 10 were waited for; matrix products, arithmetic and copies ran while one was open for 1% of the time, Pallas kernels for 0%

profile of v1, /device:TPU:24, one launch (start us, length us, event | category | flops | bytes accessed | tf_op | source)
XLA Modules:
  0.0 307.1 jit_solution(13813567811664097793)
XLA Ops:
  0.7 2.5 copy_dynamic-update-slice_fusion
  3.3 2.2 copy.58
  5.5 5.9 %all-to-all-start = ((bf16[16,2,8,40,128]{4,2,1,3,0:T(8,128)(2,1)}), bf16[16,2,8,40,128]{4,2,1,3,0:T(8,128)(2,1)}, u32[]{:S(2)}, u32[]{:S(2)}) async-start(bf16[16,2,8,40,128]{4,2,1,3,0:T(8,128)(2,1)} %bitcast.44), calls=%async_computation | async-start | bytes 5242880 | tf_op jit(solution)/shard_map/all_to_all | solution.py:190
  12.2 35.2 %all-to-all-done = bf16[16,2,8,40,128]{4,2,1,3,0:T(8,128)(2,1)} async-done(((bf16[16,2,8,40,128]{4,2,1,3,0:T(8,128)(2,1)}), bf16[16,2,8,40,128]{4,2,1,3,0:T(8,128)(2,1)}, u32[]{:S(2)}, u32[]{:S(2)}) %all-to-all-start) | async-done | bytes 2621472 | tf_op jit(solution)/shard_map/all_to_all | solution.py:190
  47.5 3.4 %slice_bitcast_fusion.1 = (bf16[16,8,40,128]{3,1,2,0:T(8,128)(2,1)}, bf16[16,8,40,128]{3,1,2,0:T(8,128)(2,1)}) fusion(bf16[16,2,8,40,128]{4,2,1,3,0:T(8,128)(2,1)} %all-to-all-done), kind=kLoop, calls=%fused_computation.9 | loop fusion | bytes 5242880 | tf_op jit(solution)/shard_map/squeeze | solution.py:195
  50.9 3.1 %gather_fusion.1 = bf16[16,8,40,128]{3,1,2,0:T(8,128)(2,1)} fusion(bf16[16,8,40,128]{3,1,2,0:T(8,128)(2,1)} %get-tuple-element.37, s32[1024]{0:T(1024)S(1)} %get-tuple-element.44), kind=kCustom, calls=%fused_computation.clone | custom fusion | bytes 2621504 | tf_op jit(solution)/shard_map/jit(_take)/gather | solution.py:195
  54.0 2.6 select_bitcast_fusion.1
  56.5 3.1 %gather_fusion.2 = bf16[16,8,40,128]{3,1,2,0:T(8,128)(2,1)} fusion(bf16[16,8,40,128]{3,1,2,0:T(8,128)(2,1)} %get-tuple-element.38, s32[1024]{0:T(1024)S(1)} %get-tuple-element.43), kind=kCustom, calls=%fused_computation.1.clone | custom fusion | bytes 2621504 | tf_op jit(solution)/shard_map/jit(_take)/gather | solution.py:195
  59.6 1.6 select_bitcast_fusion
  61.6 1.7 copy.46
  63.3 4.5 %all-to-all-start.1 = ((bf16[16,2,8,40,128]{4,2,3,1,0:T(8,128)(2,1)}), bf16[16,2,8,40,128]{4,2,3,1,0:T(8,128)(2,1)}, u32[]{:S(2)}, u32[]{:S(2)}) async-start(bf16[16,2,8,40,128]{4,2,3,1,0:T(8,128)(2,1)} %copy.46), calls=%async_computation.1 | async-start | bytes 5242880 | tf_op jit(solution)/shard_map/all_to_all | solution.py:196
  68.0 35.4 %all-to-all-done.1 = bf16[16,2,8,40,128]{4,2,3,1,0:T(8,128)(2,1)} async-done(((bf16[16,2,8,40,128]{4,2,3,1,0:T(8,128)(2,1)}), bf16[16,2,8,40,128]{4,2,3,1,0:T(8,128)(2,1)}, u32[]{:S(2)}, u32[]{:S(2)}) %all-to-all-start.1) | async-done | bytes 2621472 | tf_op jit(solution)/shard_map/all_to_all | solution.py:196
  103.5 2.5 copy.47
  110.2 3.8 %collective-permute-start = (bf16[4,2,256,128]{2,3,1,0:T(8,128)(2,1)S(1)}, bf16[4,2,256,128]{2,3,1,0:T(8,128)(2,1)S(1)}, u32[]{:S(2)}, u32[]{:S(2)}) collective-permute-start(bf16[4,2,256,128]{2,3,1,0:T(8,128)(2,1)S(1)} %bitcast.45), channel_id=1, source_target_pairs={{4,5},{5,6},{6,7},{7,8},{8,9},{9,10},{10,11},{11,12},{12,13},{13,1... | collective-permute-start | bytes 1572872 | tf_op jit(solution)/shard_map/ppermute | solution.py:205
  114.2 16.8 %collective-permute-done = bf16[4,2,256,128]{2,3,1,0:T(8,128)(2,1)S(1)} collective-permute-done((bf16[4,2,256,128]{2,3,1,0:T(8,128)(2,1)S(1)}, bf16[4,2,256,128]{2,3,1,0:T(8,128)(2,1)S(1)}, u32[]{:S(2)}, u32[]{:S(2)}) %collective-permute-start) | collective-permute-done | bytes 524320 | tf_op jit(solution)/shard_map/ppermute | solution.py:205
  131.0 1.9 collective-permute-start.1
  133.2 16.9 %collective-permute-done.1 = bf16[4,2,256,128]{2,3,1,0:T(8,128)(2,1)S(1)} collective-permute-done((bf16[4,2,256,128]{2,3,1,0:T(8,128)(2,1)S(1)}, bf16[4,2,256,128]{2,3,1,0:T(8,128)(2,1)S(1)}, u32[]{:S(2)}, u32[]{:S(2)}) %collective-permute-start.1) | collective-permute-done | bytes 524320 | tf_op jit(solution)/shard_map/ppermute | solution.py:206
  150.1 1.9 collective-permute-start.2
  152.3 16.1 %collective-permute-done.2 = bf16[4,2,256,128]{2,3,1,0:T(8,128)(2,1)S(1)} collective-permute-done((bf16[4,2,256,128]{2,3,1,0:T(8,128)(2,1)S(1)}, bf16[4,2,256,128]{2,3,1,0:T(8,128)(2,1)S(1)}, u32[]{:S(2)}, u32[]{:S(2)}) %collective-permute-start.2) | collective-permute-done | bytes 524320 | tf_op jit(solution)/shard_map/ppermute | solution.py:207
  169.9 1.9 collective-permute-start.3
  174.5 7.6 %collective-permute-done.3 = bf16[4,2,128,128]{2,3,1,0:T(8,128)(2,1)} collective-permute-done((bf16[4,2,128,128]{2,3,1,0:T(8,128)(2,1)}, bf16[4,2,128,128]{2,3,1,0:T(8,128)(2,1)}, u32[]{:S(2)}, u32[]{:S(2)}) %collective-permute-start.3) | collective-permute-done | bytes 262176 | tf_op jit(solution)/shard_map/ppermute | solution.py:208
  182.1 1.7 constant_dynamic-update-slice_fusion.4
  187.4 4.3 %copy.50.kv_ref = bf16[4,2,1152,128]{3,2,1,0:T(8,128)(2,1)} copy(bf16[4,2,1152,128]{2,3,1,0:T(8,128)(2,1)} %constant_dynamic-update-slice_fusion) | data formatting | bytes 4718592 | tf_op jit(solution)/shard_map/concatenate | solution.py:209
  193.3 55.0 %shard_map.111 = (bf16[256,4,8,128]{3,2,1,0:T(8,128)(2,1)}, bf16[256,4,8,128]{3,2,1,0:T(8,128)(2,1)}, f32[4,2,1152,128]{3,2,1,0:T(8,128)}) custom-call(bf16[256,4,8,128]{3,2,1,0:T(8,128)(2,1)S(1)} %bitcast.41, bf16[256,4,8,128]{3,2,1,0:T(8,128)(2,1)S(1)} %bitcast.42, bf16[4,2,1152,128]{3,2,1,0:T(8,128)(2,1)} %copy.50.kv_ref, ...), custom_call_target="tpu_custom_call" | custom-call | tf_op jit(solution)/shard_map/pallas_call | solution.py:117
  249.4 1.9 collective-permute-start.4
  251.3 6.3 %collective-permute-done.4 = bf16[4,2,128,128]{3,2,1,0:T(8,128)(2,1)S(1)} collective-permute-done((bf16[4,2,128,128]{3,2,1,0:T(8,128)(2,1)S(1)}, bf16[4,2,128,128]{3,2,1,0:T(8,128)(2,1)S(1)}, u32[]{:S(2)}, u32[]{:S(2)}) %collective-permute-start.4) | collective-permute-done | bytes 262176 | tf_op jit(solution)/shard_map/ppermute | solution.py:224
  259.0 5.5 %collective-permute-start.5 = (bf16[4,2,256,128]{3,2,1,0:T(8,128)(2,1)S(1)}, bf16[4,2,256,128]{3,2,1,0:T(8,128)(2,1)S(1)}, u32[]{:S(2)}, u32[]{:S(2)}) collective-permute-start(bf16[4,2,256,128]{3,2,1,0:T(8,128)(2,1)S(1)} %add_convert_fusion.3), channel_id=1, source_target_pairs={{5,4},{6,5},{7,6},{8,7},{9,8},{10,9},{11,10},{12,11},{13,12},{14,1... | collective-permute-start | bytes 1572872 | tf_op jit(solution)/shard_map/ppermute | solution.py:224
  264.5 7.3 %collective-permute-done.5 = bf16[4,2,256,128]{3,2,1,0:T(8,128)(2,1)S(1)} collective-permute-done((bf16[4,2,256,128]{3,2,1,0:T(8,128)(2,1)S(1)}, bf16[4,2,256,128]{3,2,1,0:T(8,128)(2,1)S(1)}, u32[]{:S(2)}, u32[]{:S(2)}) %collective-permute-start.5) | collective-permute-done | bytes 524320 | tf_op jit(solution)/shard_map/ppermute | solution.py:224
  273.2 8.0 %collective-permute-start.6 = (bf16[4,2,256,128]{3,2,1,0:T(8,128)(2,1)S(1)}, bf16[4,2,256,128]{3,2,1,0:T(8,128)(2,1)S(1)}, u32[]{:S(2)}, u32[]{:S(2)}) collective-permute-start(bf16[4,2,256,128]{3,2,1,0:T(8,128)(2,1)S(1)} %add_convert_fusion.2), channel_id=1, source_target_pairs={{5,4},{6,5},{7,6},{8,7},{9,8},{10,9},{11,10},{12,11},{13,12},{14,1... | collective-permute-start | bytes 1572872 | tf_op jit(solution)/shard_map/ppermute | solution.py:224
  281.2 6.7 %collective-permute-done.6 = bf16[4,2,256,128]{3,2,1,0:T(8,128)(2,1)S(1)} collective-permute-done((bf16[4,2,256,128]{3,2,1,0:T(8,128)(2,1)S(1)}, bf16[4,2,256,128]{3,2,1,0:T(8,128)(2,1)S(1)}, u32[]{:S(2)}, u32[]{:S(2)}) %collective-permute-start.6) | collective-permute-done | bytes 524320 | tf_op jit(solution)/shard_map/ppermute | solution.py:224
  289.2 8.0 %collective-permute-start.7 = (bf16[4,2,256,128]{3,2,1,0:T(8,128)(2,1)S(1)}, bf16[4,2,256,128]{3,2,1,0:T(8,128)(2,1)S(1)}, u32[]{:S(2)}, u32[]{:S(2)}) collective-permute-start(bf16[4,2,256,128]{3,2,1,0:T(8,128)(2,1)S(1)} %add_convert_fusion.1), channel_id=1, source_target_pairs={{5,4},{6,5},{7,6},{8,7},{9,8},{10,9},{11,10},{12,11},{13,12},{14,1... | collective-permute-start | bytes 1572872 | tf_op jit(solution)/shard_map/ppermute | solution.py:224
  297.2 6.7 %collective-permute-done.7 = bf16[4,2,256,128]{3,2,1,0:T(8,128)(2,1)S(1)} collective-permute-done((bf16[4,2,256,128]{3,2,1,0:T(8,128)(2,1)S(1)}, bf16[4,2,256,128]{3,2,1,0:T(8,128)(2,1)S(1)}, u32[]{:S(2)}, u32[]{:S(2)}) %collective-permute-start.7) | collective-permute-done | bytes 524320 | tf_op jit(solution)/shard_map/ppermute | solution.py:224
  (94 shorter events, 23.9 us)
Async XLA Ops:
  0.6 2.5 copy-start.10
  0.6 2.6 copy-start.11
  5.5 5.9 %copy-start.13 = (s32[16,11]{1,0:T(8,128)S(1)}, s32[16,11]{1,0:T(8,128)}, u32[]{:S(2)}) copy-start(s32[16,11]{1,0:T(8,128)} %param.17) | copy-start | bytes 2116
  5.5 42.0 %all-to-all-start = ((bf16[16,2,8,40,128]{4,2,1,3,0:T(8,128)(2,1)}), bf16[16,2,8,40,128]{4,2,1,3,0:T(8,128)(2,1)}, u32[]{:S(2)}, u32[]{:S(2)}) async-start(bf16[16,2,8,40,128]{4,2,1,3,0:T(8,128)(2,1)} %bitcast.44), calls=%async_computation | async-start | bytes 5242880 | tf_op jit(solution)/shard_map/all_to_all | solution.py:190
  59.6 1.7 copy-start.3
  63.3 4.5 %copy-start.12 = (f32[16,11]{1,0:T(8,128)S(1)}, f32[16,11]{1,0:T(8,128)}, u32[]{:S(2)}) copy-start(f32[16,11]{1,0:T(8,128)} %param.14) | copy-start | bytes 2116
  63.3 40.1 %all-to-all-start.1 = ((bf16[16,2,8,40,128]{4,2,3,1,0:T(8,128)(2,1)}), bf16[16,2,8,40,128]{4,2,3,1,0:T(8,128)(2,1)}, u32[]{:S(2)}, u32[]{:S(2)}) async-start(bf16[16,2,8,40,128]{4,2,3,1,0:T(8,128)(2,1)} %copy.46), calls=%async_computation.1 | async-start | bytes 5242880 | tf_op jit(solution)/shard_map/all_to_all | solution.py:196
  105.9 8.1 %copy-start.14 = (s32[16,11]{1,0:T(8,128)S(1)}, s32[16,11]{1,0:T(8,128)}, u32[]{:S(2)}) copy-start(s32[16,11]{1,0:T(8,128)} %param.15) | copy-start | bytes 2116
  105.9 8.1 %copy-start.15 = (s32[16,11]{1,0:T(8,128)S(1)}, s32[16,11]{1,0:T(8,128)}, u32[]{:S(2)}) copy-start(s32[16,11]{1,0:T(8,128)} %param.16) | copy-start | bytes 2116
  106.4 1.5 copy-start.1
  108.8 64.2 %copy-start.2 = (bf16[256,40,128]{2,0,1:T(8,128)(2,1)S(1)}, bf16[256,40,128]{2,0,1:T(8,128)(2,1)}, u32[]{:S(2)}) copy-start(bf16[256,40,128]{2,0,1:T(8,128)(2,1)} %copy-done.1) | copy-start | bytes 7864324
  110.2 20.8 %collective-permute-start = (bf16[4,2,256,128]{2,3,1,0:T(8,128)(2,1)S(1)}, bf16[4,2,256,128]{2,3,1,0:T(8,128)(2,1)S(1)}, u32[]{:S(2)}, u32[]{:S(2)}) collective-permute-start(bf16[4,2,256,128]{2,3,1,0:T(8,128)(2,1)S(1)} %bitcast.45), channel_id=1, source_target_pairs={{4,5},{5,6},{6,7},{7,8},{8,9},{9,10},{10,11},{11,12},{12,13},{13,1... | collective-permute-start | bytes 1572872 | tf_op jit(solution)/shard_map/ppermute | solution.py:205
  131.0 2.2 copy-start.6
  131.0 19.1 %collective-permute-start.1 = (bf16[4,2,256,128]{2,3,1,0:T(8,128)(2,1)S(1)}, bf16[4,2,256,128]{2,3,1,0:T(8,128)(2,1)S(1)}, u32[]{:S(2)}, u32[]{:S(2)}) collective-permute-start(bf16[4,2,256,128]{2,3,1,0:T(8,128)(2,1)S(1)} %collective-permute-done), channel_id=1, source_target_pairs={{4,5},{5,6},{6,7},{7,8},{8,9},{9,10},{10,11},{11,12},{12,13},{13,1... | collective-permute-start | bytes 1572872 | tf_op jit(solution)/shard_map/ppermute | solution.py:206
  150.1 19.8 %copy-start.8 = (bf16[4,2,256,128]{2,3,1,0:T(8,128)(2,1)}, bf16[4,2,256,128]{2,3,1,0:T(8,128)(2,1)S(1)}, u32[]{:S(2)}) copy-start(bf16[4,2,256,128]{2,3,1,0:T(8,128)(2,1)S(1)} %collective-permute-done.1) | copy-start | bytes 1572868
  150.1 18.3 %collective-permute-start.2 = (bf16[4,2,256,128]{2,3,1,0:T(8,128)(2,1)S(1)}, bf16[4,2,256,128]{2,3,1,0:T(8,128)(2,1)S(1)}, u32[]{:S(2)}, u32[]{:S(2)}) collective-permute-start(bf16[4,2,256,128]{2,3,1,0:T(8,128)(2,1)S(1)} %collective-permute-done.1), channel_id=1, source_target_pairs={{4,5},{5,6},{6,7},{7,8},{8,9},{9,10},{10,11},{11,12},{12,13},{13,1... | collective-permute-start | bytes 1572872 | tf_op jit(solution)/shard_map/ppermute | solution.py:207
  168.4 0.8 copy-start.4
  169.9 12.2 %collective-permute-start.3 = (bf16[4,2,128,128]{2,3,1,0:T(8,128)(2,1)}, bf16[4,2,128,128]{2,3,1,0:T(8,128)(2,1)}, u32[]{:S(2)}, u32[]{:S(2)}) collective-permute-start(bf16[4,2,128,128]{2,3,1,0:T(8,128)(2,1)} %slice.91), channel_id=1, source_target_pairs={{4,5},{5,6},{6,7},{7,8},{8,9},{9,10},{10,11},{11,12},{12,13},{13,1... | collective-permute-start | bytes 786440 | tf_op jit(solution)/shard_map/ppermute | solution.py:208
  173.2 10.7 %copy-start.5 = (bf16[4,2,256,128]{2,3,1,0:T(8,128)(2,1)S(1)}, bf16[4,2,256,128]{2,3,1,0:T(8,128)(2,1)}, u32[]{:S(2)}) copy-start(bf16[4,2,256,128]{2,3,1,0:T(8,128)(2,1)} %copy-done.4) | copy-start | bytes 1572868
  173.2 11.6 %copy-start.9 = (bf16[4,2,256,128]{2,3,1,0:T(8,128)(2,1)S(1)}, bf16[4,2,256,128]{2,3,1,0:T(8,128)(2,1)}, u32[]{:S(2)}) copy-start(bf16[4,2,256,128]{2,3,1,0:T(8,128)(2,1)} %copy-done.8) | copy-start | bytes 1572868
  174.5 11.1 %copy-start.7 = (bf16[4,2,256,128]{2,3,1,0:T(8,128)(2,1)S(1)}, bf16[4,2,256,128]{2,3,1,0:T(8,128)(2,1)}, u32[]{:S(2)}) copy-start(bf16[4,2,256,128]{2,3,1,0:T(8,128)(2,1)} %copy-done.6) | copy-start | bytes 1572868
  191.7 1.6 copy-start
  249.4 8.3 %collective-permute-start.4 = (bf16[4,2,128,128]{3,2,1,0:T(8,128)(2,1)S(1)}, bf16[4,2,128,128]{3,2,1,0:T(8,128)(2,1)S(1)}, u32[]{:S(2)}, u32[]{:S(2)}) collective-permute-start(bf16[4,2,128,128]{3,2,1,0:T(8,128)(2,1)S(1)} %slice.120), channel_id=1, source_target_pairs={{5,4},{6,5},{7,6},{8,7},{9,8},{10,9},{11,10},{12,11},{13,12},{14,1... | collective-permute-start | bytes 786440 | tf_op jit(solution)/shard_map/ppermute | solution.py:224
  259.0 12.9 %collective-permute-start.5 = (bf16[4,2,256,128]{3,2,1,0:T(8,128)(2,1)S(1)}, bf16[4,2,256,128]{3,2,1,0:T(8,128)(2,1)S(1)}, u32[]{:S(2)}, u32[]{:S(2)}) collective-permute-start(bf16[4,2,256,128]{3,2,1,0:T(8,128)(2,1)S(1)} %add_convert_fusion.3), channel_id=1, source_target_pairs={{5,4},{6,5},{7,6},{8,7},{9,8},{10,9},{11,10},{12,11},{13,12},{14,1... | collective-permute-start | bytes 1572872 | tf_op jit(solution)/shard_map/ppermute | solution.py:224
  273.2 14.7 %collective-permute-start.6 = (bf16[4,2,256,128]{3,2,1,0:T(8,128)(2,1)S(1)}, bf16[4,2,256,128]{3,2,1,0:T(8,128)(2,1)S(1)}, u32[]{:S(2)}, u32[]{:S(2)}) collective-permute-start(bf16[4,2,256,128]{3,2,1,0:T(8,128)(2,1)S(1)} %add_convert_fusion.2), channel_id=1, source_target_pairs={{5,4},{6,5},{7,6},{8,7},{9,8},{10,9},{11,10},{12,11},{13,12},{14,1... | collective-permute-start | bytes 1572872 | tf_op jit(solution)/shard_map/ppermute | solution.py:224
  289.2 14.7 %collective-permute-start.7 = (bf16[4,2,256,128]{3,2,1,0:T(8,128)(2,1)S(1)}, bf16[4,2,256,128]{3,2,1,0:T(8,128)(2,1)S(1)}, u32[]{:S(2)}, u32[]{:S(2)}) collective-permute-start(bf16[4,2,256,128]{3,2,1,0:T(8,128)(2,1)S(1)} %add_convert_fusion.1), channel_id=1, source_target_pairs={{5,4},{6,5},{7,6},{8,7},{9,8},{10,9},{11,10},{12,11},{13,12},{14,1... | collective-permute-start | bytes 1572872 | tf_op jit(solution)/shard_map/ppermute | solution.py:224

commit v2 on v1

v2 whole, which is shorter than its diff:
```python
import functools

import jax
import jax.numpy as jnp
from jax import lax
from jax.experimental import pallas as pl
from jax.experimental.pallas import tpu as pltpu
from jax.sharding import PartitionSpec as P

DH = 128
BLK = 128
SHORTS = 8
WINDOW = 9 * BLK
OWN = 7 * BLK
TILE = 256
CHUNK = 256
NEVER = 1 << 20
SCALE = DH**-0.5
EXP_SCALE = SCALE * 1.4426950408889634
NT = (((1,), (1,)), ((), ()))
NN = (((1,), (0,)), ((), ()))
MESH = pl.DeviceIdType.MESH


def dot(a, b, dims):
    return lax.dot_general(a, b, dims, preferred_element_type=jnp.float32)


def attend_tile(q, up, start, token, live, weight, k, v, kt, vt, add_dk, add_dv, s_ref, p_ref, key0, chunk, chunks):
    rows = q.shape[0]
    highest = jnp.full((1, rows), -1e30, jnp.float32)
    for c in range(chunks):
        s = dot(k(c), q, NT)
        key = key0 + c * chunk + lax.broadcasted_iota(jnp.int32, (chunk, rows), 0)
        allowed = key >= start
        if c == chunks - 1:
            allowed = allowed & (key <= token)
        s = jnp.where(allowed, s, -1e30)
        s_ref[c, :chunk] = s
        highest = jnp.maximum(highest, jnp.max(s, axis=0, keepdims=True))
    shift = highest * EXP_SCALE
    total = jnp.zeros((1, rows), jnp.float32)
    out_t = jnp.zeros((DH, rows), jnp.float32)
    for c in range(chunks):
        p = jnp.exp2(s_ref[c, :chunk] * EXP_SCALE - shift)
        total = total + jnp.sum(p, axis=0, keepdims=True)
        p16 = p.astype(jnp.bfloat16)
        p_ref[c, :chunk] = p16
        out_t = out_t + dot(vt(c), p16, NN)
    out_t = out_t * (live / total)
    scaled = up.astype(jnp.float32).T * (weight / total)
    delta = jnp.sum(scaled * out_t, axis=0, keepdims=True)
    scaled16 = scaled.astype(jnp.bfloat16)
    dq_t = jnp.zeros((DH, rows), jnp.float32)
    for c in range(chunks):
        p16 = p_ref[c, :chunk]
        gp = dot(v(c), scaled16, NN)
        ds = (p16.astype(jnp.float32) * (gp - delta)).astype(jnp.bfloat16)
        add_dv(c, dot(p16, scaled16, NT))
        add_dk(c, dot(ds, q, NN))
        dq_t = dq_t + dot(kt(c), ds, NN)
    return out_t.T, (dq_t * SCALE).T


def kernel(groups, seq_count, short_rows, q_hbm, up_hbm, kv_hbm, src_ref, rows_i, rows_f, o_ref, dq_ref, dkv_ref,
           q_v, up_v, kw, kt, dkv, s_ref, p_ref, sbuf, rbuf,
           r1q0, r1q1, s2q0, s2q1, r1k0, r1k1, s2k0, s2k1,
           load_sem, gather_send, gather_recv, chain_send, chain_recv, x_send, x_recv):
    seq = lax.axis_index("seq")
    dp = lax.axis_index("dp")
    tokens, kv_count, per, _ = q_v.shape
    step_tokens = TILE // per
    tiles = tokens // step_tokens
    here = tokens // BLK
    is_long = seq >= short_rows
    has_prev = seq > short_rows
    has_next = (seq >= short_rows) & (seq < seq_count - 1)

    barrier = pltpu.get_barrier_semaphore()

    @pl.when(has_prev)
    def _():
        pl.semaphore_signal(barrier, inc=1, device_id={"seq": seq - 1}, device_id_type=MESH)

    @pl.when(has_next)
    def _():
        pl.semaphore_signal(barrier, inc=1, device_id={"seq": seq + 1}, device_id_type=MESH)

    @pl.when(jnp.logical_not(is_long))
    def _():
        def greet(r, _):
            pl.semaphore_signal(barrier, inc=1, device_id={"dp": lax.rem(dp + r, groups)}, device_id_type=MESH)
            return 0

        lax.fori_loop(1, groups, greet, 0)
        pl.semaphore_wait(barrier, groups - 1)

    @pl.when(has_prev & has_next)
    def _():
        pl.semaphore_wait(barrier, 2)

    @pl.when(has_prev != has_next)
    def _():
        pl.semaphore_wait(barrier, 1)

    def tile(g, i, k, v, kt_of, vt_of, add_dk, add_dv, key0, chunk, chunks):
        spot = pl.ds(pl.multiple_of(i * step_tokens, step_tokens), step_tokens)
        q = q_v[spot, g].astype(jnp.float32).reshape(TILE, DH).astype(jnp.bfloat16)
        up = up_v[spot, g].astype(jnp.float32).reshape(TILE, DH)
        out, dq = attend_tile(
            q, up, rows_i[0, pl.ds(i, 1), :], rows_i[1, pl.ds(i, 1), :], rows_f[0, pl.ds(i, 1), :], rows_f[1, pl.ds(i, 1), :],
            k, v, kt_of, vt_of, add_dk, add_dv, s_ref, p_ref, key0, chunk, chunks,
        )
        o_ref[spot, g] = out.reshape(step_tokens, per, DH).astype(jnp.bfloat16)
        dq_ref[spot, g] = dq.reshape(step_tokens, per, DH).astype(jnp.bfloat16)

    up_load = pltpu.make_async_copy(up_hbm, up_v, load_sem.at[0])
    up_load.start()

    @pl.when(is_long)
    def _():
        q_load = pltpu.make_async_copy(q_hbm, q_v, load_sem.at[1])
        kv_load = pltpu.make_async_copy(kv_hbm, kw.at[:, :, pl.ds(OWN, tokens)], load_sem.at[2])
        kv_load.start()
        q_load.start()

        @pl.when(jnp.logical_not(has_prev))
        def _():
            kw[:, :, :OWN] = jnp.zeros((kv_count, 2, OWN, DH), kw.dtype)

        kv_load.wait()
        hop_from = (OWN, OWN - tokens, OWN - 2 * tokens, BLK * 2)
        hop_to = (OWN - tokens, OWN - 2 * tokens, OWN - 3 * tokens, 0)
        hop_rows = (tokens, tokens, tokens, BLK)

        def gather(g, k):
            return pltpu.make_async_remote_copy(
                src_ref=kw.at[g, :, pl.ds(hop_from[k], hop_rows[k])],
                dst_ref=kw.at[g, :, pl.ds(hop_to[k], hop_rows[k])],
                send_sem=gather_send.at[g, k],
                recv_sem=gather_recv.at[g, k],
                device_id={"seq": seq + 1},
                device_id_type=MESH,
            )

        def gather_arrived(g, k, when=True):
            @pl.when(has_prev & when)
            def _():
                gather(g, k).wait_recv()

        def gather_step(g, k, when=True):
            if k > 0:
                gather_arrived(g, k - 1, when)

            @pl.when(has_next & when)
            def _():
                gather(g, k).start()

        part_at = (0, BLK, 3 * BLK, 5 * BLK, 7 * BLK)
        part_rows = (BLK, tokens, tokens, tokens, tokens)

        def chain(g, k):
            return pltpu.make_async_remote_copy(
                src_ref=sbuf.at[g, k, :, pl.ds(0, part_rows[k])],
                dst_ref=rbuf.at[g, k, :, pl.ds(0, part_rows[k])],
                send_sem=chain_send.at[g, k],
                recv_sem=chain_recv.at[g, k],
                device_id={"seq": seq - 1},
                device_id_type=MESH,
            )

        def chain_step(g, k, when=True):
            if k > 0:
                @pl.when(has_next & when)
                def _():
                    chain(g, k - 1).wait_recv()
                    got = part_rows[k - 1]
                    at = pl.ds(part_at[k] + tokens - got, got)
                    dkv[g, :, at] += rbuf[g, k - 1, :, :got].astype(jnp.float32)

            if k < 4:
                @pl.when(has_prev & when)
                def _():
                    sbuf[g, k, :, : part_rows[k]] = dkv[g, :, pl.ds(part_at[k], part_rows[k])].astype(jnp.bfloat16)
                    chain(g, k).start()
            else:
                @pl.when(when)
                def _():
                    dkv_ref[g, 0] = (dkv[g, 0, pl.ds(OWN, tokens)] * SCALE).astype(jnp.bfloat16)
                    dkv_ref[g, 1] = dkv[g, 1, pl.ds(OWN, tokens)].astype(jnp.bfloat16)

        gather_step(0, 0)
        gather_step(0, 1)
        gather_step(0, 2)
        gather_step(1, 0)
        gather_step(0, 3)
        gather_step(1, 1)
        dkv[...] = jnp.zeros_like(dkv)
        q_load.wait()
        up_load.wait()
        gather_arrived(0, 3)

        def turn(t, _):
            g = t // tiles
            i = lax.rem(t, tiles)

            @pl.when(i == 0)
            def _():
                kt[0] = kw[g, 0].T
                kt[1] = kw[g, 1].T

            before, after, later = jnp.maximum(g - 1, 0), jnp.minimum(g + 1, kv_count - 1), jnp.minimum(g + 2, kv_count - 1)
            for k in range(1, 5):
                chain_step(before, k, (g > 0) & (i == 2 * k - 1))
            gather_step(after, 2, (g < kv_count - 1) & (i == 1))
            gather_step(later, 0, (g < kv_count - 2) & (i == 1))
            gather_step(after, 3, (g < kv_count - 1) & (i == 4))
            gather_step(later, 1, (g < kv_count - 2) & (i == 4))

            off = pl.multiple_of((i // (tiles // here)) * BLK, BLK)

            def at(c):
                return pl.ds(pl.multiple_of(off + c * CHUNK, BLK), CHUNK)

            def add(which):
                def one(c, value):
                    dkv[g, which, at(c)] += value

                return one

            tile(g, i, lambda c: kw[g, 0, at(c)], lambda c: kw[g, 1, at(c)], lambda c: kt[0, :, at(c)], lambda c: kt[1, :, at(c)],
                 add(0), add(1), off, CHUNK, (WINDOW - BLK) // CHUNK)

            chain_step(g, 0, i == tiles - 1)
            gather_arrived(after, 3, (g < kv_count - 1) & (i == tiles - 1))
            return 0

        lax.fori_loop(0, kv_count * tiles, turn, 0)
        for k in range(1, 5):
            chain_step(kv_count - 1, k)
        for g in range(kv_count):
            for k in range(4):
                @pl.when(has_next)
                def _():
                    gather(g, k).wait_send()

                @pl.when(has_prev)
                def _():
                    chain(g, k).wait_send()

    @pl.when(jnp.logical_not(is_long))
    def _():
        r1q, s2q, r1k, s2k = (r1q0, r1q1), (s2q0, s2q1), (r1k0, r1k1), (s2k0, s2k1)
        piece = BLK // groups
        parts = groups // (2 * kv_count)
        kv_piece = BLK // parts

        def kv_spot(ref, m, i):
            head = m // (2 * parts)
            which = lax.rem(m // parts, 2)
            return ref.at[head, which, pl.ds(pl.multiple_of(i * BLK + lax.rem(m, parts) * kv_piece, kv_piece), kv_piece)]

        def q_spot(ref, m, i):
            return ref.at[pl.ds(pl.multiple_of(i * BLK + m * piece, piece), piece)]

        def remote(src, dst, n, d):
            return pltpu.make_async_remote_copy(
                src_ref=src, dst_ref=dst, send_sem=x_send.at[n], recv_sem=x_recv.at[n], device_id={"dp": d}, device_id_type=MESH
            )

        for i in range(here):
            pltpu.make_async_copy(q_spot(q_hbm, dp, i), r1q[i].at[dp], x_recv.at[4 * i]).start()
            pltpu.make_async_copy(kv_spot(kv_hbm, dp, i), r1k[i].at[dp], x_recv.at[4 * i + 1]).start()

            def spread(r, _):
                d = lax.rem(dp + r, groups)
                remote(q_spot(q_hbm, d, i), r1q[i].at[dp], 4 * i, d).start()
                remote(kv_spot(kv_hbm, d, i), r1k[i].at[dp], 4 * i + 1, d).start()
                return 0

            lax.fori_loop(1, groups, spread, 0)

        for i in range(here):
            pltpu.make_async_copy(r1q[i], r1q[i], x_recv.at[4 * i]).wait()
            pltpu.make_async_copy(r1k[i], r1k[i], x_recv.at[4 * i + 1]).wait()

            def relay(r, _):
                d = lax.rem(dp + r, groups)
                source = src_ref[i, d]
                s2q[i][d] = r1q[i][source]
                s2k[i][d] = r1k[i][source]
                remote(s2q[i].at[d], q_spot(q_v, dp, i), 4 * i + 2, d).start()
                remote(s2k[i].at[d], kv_spot(kw, dp, i), 4 * i + 3, d).start()
                return 0

            lax.fori_loop(1, groups, relay, 0)
            source = src_ref[i, dp]
            q_v[pl.ds(pl.multiple_of(i * BLK + dp * piece, piece), piece)] = r1q[i][source]
            mine = dp // (2 * parts), lax.rem(dp // parts, 2), pl.multiple_of(i * BLK + lax.rem(dp, parts) * kv_piece, kv_piece)
            kw[mine[0], mine[1], pl.ds(mine[2], kv_piece)] = r1k[i][source]

        up_load.wait()
        most = pl.ds(0, groups - 1)
        for i in range(here):
            pltpu.make_async_copy(s2q[i].at[most], s2q[i].at[most], x_recv.at[4 * i + 2]).wait()
            pltpu.make_async_copy(s2k[i].at[most], s2k[i].at[most], x_recv.at[4 * i + 3]).wait()
            at = pl.ds(i * BLK, BLK)
            share = tiles // here

            def small(t, _):
                g = t // share
                n = i * share + lax.rem(t, share)

                @pl.when(lax.rem(t, share) == 0)
                def _():
                    kt[0, :, :BLK] = kw[g, 0, at].T
                    kt[1, :, :BLK] = kw[g, 1, at].T
                    dkv[g, :, at] = jnp.zeros((2, BLK, DH), jnp.float32)

                def add(which):
                    def one(c, value):
                        dkv[g, which, at] += value

                    return one

                tile(g, n, lambda c: kw[g, 0, at], lambda c: kw[g, 1, at], lambda c: kt[0, :, :BLK], lambda c: kt[1, :, :BLK],
                     add(0), add(1), i * BLK, BLK, 1)

                @pl.when(lax.rem(t, share) == share - 1)
                def _():
                    dkv_ref[g, 0, at] = (dkv[g, 0, at] * SCALE).astype(jnp.bfloat16)
                    dkv_ref[g, 1, at] = dkv[g, 1, at].astype(jnp.bfloat16)

                return 0

            lax.fori_loop(0, kv_count * share, small, 0)
        for i in range(here):
            for phase in range(2):
                pltpu.make_async_copy(s2q[i].at[most], s2q[i].at[most], x_send.at[4 * i + 2 * phase]).wait()
                pltpu.make_async_copy(s2k[i].at[most], s2k[i].at[most], x_send.at[4 * i + 2 * phase + 1]).wait()


def attention(q, up, kv, source, rows_i, rows_f, groups, seq_count, short_rows):
    tokens, kv_count, per, _ = q.shape
    half = jnp.bfloat16
    piece = BLK // groups
    kv_piece = BLK // (groups // (2 * kv_count))
    any_spec = pl.BlockSpec(memory_space=pl.ANY)
    vmem = pl.BlockSpec(memory_space=pltpu.VMEM)
    q_pieces = pltpu.VMEM((groups, piece, kv_count, per, DH), half)
    kv_pieces = pltpu.VMEM((groups, kv_piece, DH), half)
    chunks = (WINDOW - BLK) // CHUNK
    return pl.pallas_call(
        functools.partial(kernel, groups, seq_count, short_rows),
        in_specs=[any_spec, any_spec, any_spec, pl.BlockSpec(memory_space=pltpu.SMEM), vmem, vmem],
        out_specs=[vmem, vmem, vmem],
        out_shape=[
            jax.ShapeDtypeStruct(q.shape, half),
            jax.ShapeDtypeStruct(q.shape, half),
            jax.ShapeDtypeStruct(kv.shape, half),
        ],
        scratch_shapes=[
            pltpu.VMEM(q.shape, half),
            pltpu.VMEM(q.shape, half),
            pltpu.VMEM((kv_count, 2, WINDOW, DH), half),
            pltpu.VMEM((2, DH, WINDOW), half),
            pltpu.VMEM((kv_count, 2, WINDOW, DH), jnp.float32),
            pltpu.VMEM((chunks, CHUNK, TILE), jnp.float32),
            pltpu.VMEM((chunks, CHUNK, TILE), half),
            pltpu.VMEM((kv_count, 4, 2, tokens, DH), half),
            pltpu.VMEM((kv_count, 4, 2, tokens, DH), half),
            q_pieces, q_pieces, q_pieces, q_pieces,
            kv_pieces, kv_pieces, kv_pieces, kv_pieces,
            pltpu.SemaphoreType.DMA((3,)),
            pltpu.SemaphoreType.DMA((kv_count, 4)),
            pltpu.SemaphoreType.DMA((kv_count, 4)),
            pltpu.SemaphoreType.DMA((kv_count, 4)),
            pltpu.SemaphoreType.DMA((kv_count, 4)),
            pltpu.SemaphoreType.DMA((8,)),
            pltpu.SemaphoreType.DMA((8,)),
        ],
        compiler_params=pltpu.CompilerParams(
            collective_id=0, has_side_effects=True, vmem_limit_bytes=52 * 1024 * 1024
        ),
    )(q, up, kv, source, rows_i, rows_f)


def row_tables(rewards, response_length, block_start, move_plan, own_group, position):
    groups = rewards.shape[0]
    advantage = rewards - jnp.mean(rewards, axis=1, keepdims=True)
    every = jnp.arange(groups, dtype=jnp.int32)[:, None]
    owner = jnp.concatenate([move_plan[:, :SHORTS], jnp.broadcast_to(every, (groups, rewards.shape[1] - SHORTS))], axis=1)
    mine = owner == own_group
    starts = jnp.sum(jnp.where(mine, block_start, 0), axis=0) * BLK
    ends = starts + jnp.sum(jnp.where(mine, response_length, 0), axis=0)
    advs = jnp.sum(jnp.where(mine, advantage, 0.0), axis=0)
    inside = (position[None, :] >= starts[:, None]) & (position[None, :] < ends[:, None])
    live = jnp.sum(inside.astype(jnp.float32), axis=0)
    start = jnp.sum(jnp.where(inside, starts[:, None], 0), axis=0)
    weight = jnp.sum(jnp.where(inside, advs[:, None], 0.0), axis=0)
    return live, start, weight


def body(queries, keys, values, upstream, rewards, response_length, block_start, move_plan):
    groups = lax.axis_size("dp")
    seq_count = lax.axis_size("seq")
    own_group = lax.axis_index("dp")
    own_seq = lax.axis_index("seq")
    tokens, heads, _ = queries.shape
    kv_count = keys.shape[1]
    per = heads // kv_count
    here = tokens // BLK
    short_rows = SHORTS // here

    slots = jnp.minimum(own_seq * here, SHORTS - here)
    chosen = lax.dynamic_slice_in_dim(move_plan, slots, here, axis=1)
    every = jnp.arange(groups, dtype=jnp.int32)
    source = jnp.sum(
        jnp.where(chosen.T[:, :, None] == every[None, None, :], every[None, :, None], 0), axis=1
    )

    tiles = tokens * per // TILE
    token = jnp.arange(tokens * per, dtype=jnp.int32) // per
    position = own_seq * tokens + token
    live, start, weight = row_tables(rewards, response_length, block_start, move_plan, own_group, position)
    base = own_seq * tokens - jnp.where(own_seq < short_rows, 0, OWN)
    start_w = jnp.where(live > 0, start - base, NEVER)
    rows_i = jnp.stack([start_w, position - base]).reshape(2, tiles, TILE)
    rows_f = jnp.stack([live, weight]).reshape(2, tiles, TILE)

    q = queries.reshape(tokens, kv_count, per, DH)
    up = upstream.reshape(tokens, kv_count, per, DH)
    kv = jnp.stack([keys, values]).transpose(2, 0, 1, 3)
    out, dq, grads = attention(q, up, kv, source, rows_i, rows_f, groups, seq_count, short_rows)
    grads = grads.transpose(1, 2, 0, 3)
    return (out.reshape(queries.shape), dq.reshape(queries.shape), grads[0], grads[1])


def solution(mesh):
    spec = P(("dp", "seq"), None, None)
    return jax.shard_map(
        body,
        mesh=mesh,
        in_specs=(spec,) * 4 + (P(),) * 4,
        out_specs=(spec,) * 4,
        check_vma=False,
    )
```

time: 308 us -> 144 us (0.47)
  the two profiles are of different devices: /device:TPU:24 before, /device:TPU:134 now
where the time goes in v2:
time: 144 us; the launch traced here: 142 us
  Pallas kernels  131 us (91%)
  local copies, waits for them, and re-layouts  7.49 us (5%)
  other arithmetic  2.78 us (2%)
    pallas_call x1, Pallas kernels, attention(): pl.pallas_call(functools.partial(kernel, groups, seq_count, short_rows),...  131 us
    unnamed x8, local copies, waits for them, and re-layouts  5.48 us

profile of v2, /device:TPU:134, one launch (start us, length us, event | category | flops | bytes accessed | tf_op | source)
XLA Modules:
  0.0 141.8 jit_solution(3339744064571485660)
XLA Ops:
  0.6 0.8 reduce_sum.80
  1.5 0.8 dynamic-slice_bitcast_fusion
  2.2 0.1 copy.19
  2.3 0.1 select_reduce_fusion.2.src_ref
  2.4 0.8 select_reduce_fusion.3
  3.2 0.7 select_reduce_fusion.5
  4.0 0.1 select_reduce_fusion.1
  4.1 0.1 select_reduce_fusion
  4.3 1.1 copy_bitcast_fusion
  5.4 0.1 maximum_bitcast_fusion.kv_hbm
  5.5 130.8 %shard_map.111 = (bf16[256,4,8,128]{3,2,1,0:T(8,128)(2,1)}, bf16[256,4,8,128]{3,2,1,0:T(8,128)(2,1)}, bf16[4,2,256,128]{3,2,1,0:T(8,128)(2,1)S(1)}) custom-call(bf16[256,4,8,128]{3,2,1,0:T(8,128)(2,1)} %bitcast.21, bf16[256,4,8,128]{3,2,1,0:T(8,128)(2,1)} %bitcast.22, bf16[4,2,256,128]{3,2,1,0:T(8,128)(2,1)S(1)} %maximum_bitcast_fusion.kv_hbm, ...), custom_call_target="tpu_custom_call" | custom-call | tf_op jit(solution)/shard_map/pallas_call | solution.py:353
  136.3 0.0 copy-start.1
  136.4 0.9 copy.21
  137.3 0.9 copy.20
  138.2 0.0 copy-done.1
  138.2 0.0 copy-start
  138.2 1.3 copy.26
  139.5 1.0 copy-done
  140.5 1.3 copy.27
  (12 shorter events, 0.1 us)
Async XLA Ops:
  136.3 1.9 %copy-start.1 = (bf16[256,4,8,128]{3,2,1,0:T(8,128)(2,1)S(1)}, bf16[256,4,8,128]{3,2,1,0:T(8,128)(2,1)}, u32[]{:S(2)}) copy-start(bf16[256,4,8,128]{3,2,1,0:T(8,128)(2,1)} %get-tuple-element.7) | copy-start | bytes 6291460
  138.2 2.3 %copy-start = (bf16[256,4,8,128]{3,2,1,0:T(8,128)(2,1)S(1)}, bf16[256,4,8,128]{3,2,1,0:T(8,128)(2,1)}, u32[]{:S(2)}) copy-start(bf16[256,4,8,128]{3,2,1,0:T(8,128)(2,1)} %get-tuple-element.8) | copy-start | bytes 6291460

commit v3 on v2

v3 whole, which is shorter than its diff:
```python
import functools

import jax
import jax.numpy as jnp
from jax import lax
from jax.experimental import pallas as pl
from jax.experimental.pallas import tpu as pltpu
from jax.sharding import PartitionSpec as P

DH = 128
BLK = 128
SHORTS = 8
WINDOW = 9 * BLK
OWN = 7 * BLK
CHUNK = 256
NEVER = 1 << 20
SCALE = DH**-0.5
EXP_SCALE = SCALE * 1.4426950408889634
NT = (((1,), (1,)), ((), ()))
NN = (((1,), (0,)), ((), ()))
MESH = pl.DeviceIdType.MESH


def dot(a, b, dims):
    return lax.dot_general(a, b, dims, preferred_element_type=jnp.float32)


def attend_tile(q, up, start, token, live, weight, k, v, kt, vt, add_dk, add_dv, s_ref, p_ref, key0, chunk, chunks, hook):
    rows = q.shape[0]
    hook(0)
    highest = jnp.full((1, rows), -1e30, jnp.float32)
    for c in range(chunks):
        s = dot(k(c), q, NT)
        key = key0 + c * chunk + lax.broadcasted_iota(jnp.int32, (chunk, rows), 0)
        allowed = key >= start
        if c == chunks - 1:
            allowed = allowed & (key <= token)
        s = jnp.where(allowed, s, -1e30)
        s_ref[c, :chunk] = s
        highest = jnp.maximum(highest, jnp.max(s, axis=0, keepdims=True))
    hook(1)
    shift = highest * EXP_SCALE
    total = jnp.zeros((1, rows), jnp.float32)
    out_t = jnp.zeros((DH, rows), jnp.float32)
    for c in range(chunks):
        p = jnp.exp2(s_ref[c, :chunk] * EXP_SCALE - shift)
        total = total + jnp.sum(p, axis=0, keepdims=True)
        p16 = p.astype(jnp.bfloat16)
        p_ref[c, :chunk] = p16
        out_t = out_t + dot(vt(c), p16, NN)
    hook(2)
    out_t = out_t * (live / total)
    scaled = up.astype(jnp.float32).T * (weight / total)
    delta = jnp.sum(scaled * out_t, axis=0, keepdims=True)
    scaled16 = scaled.astype(jnp.bfloat16)
    dq_t = jnp.zeros((DH, rows), jnp.float32)
    for c in range(chunks):
        p16 = p_ref[c, :chunk]
        gp = dot(v(c), scaled16, NN)
        ds = (p16.astype(jnp.float32) * (gp - delta)).astype(jnp.bfloat16)
        add_dv(c, dot(p16, scaled16, NT))
        add_dk(c, dot(ds, q, NN))
        dq_t = dq_t + dot(kt(c), ds, NN)
    return out_t.T, (dq_t * SCALE).T


def kernel(groups, seq_count, short_rows, boundary, q_hbm, up_hbm, kv_hbm, reward_ref, length_ref, block_ref, plan_ref,
           o_ref, dq_ref, dkv_ref,
           q_v, up_v, kw, relay_v, kt, dkv, s_ref, p_ref, sbuf, rbuf,
           r1q0, r1q1, s2q0, s2q1, r1k0, r1k1, s2k0, s2k1, source_ref,
           load_sem, gather_send, gather_recv, relay_recv, chain_send, chain_recv, x_send, x_recv):
    seq = lax.axis_index("seq")
    dp = lax.axis_index("dp")
    tokens, kv_count, per, _ = q_v.shape
    tile_rows = BLK * per
    here = tokens // BLK
    rolls = reward_ref.shape[1]
    last = seq_count - 1
    is_long = seq >= short_rows
    has_prev = seq > short_rows
    has_next = is_long & (seq < last)
    is_edge = seq == boundary - 1
    is_relay = seq == last
    plain_next = has_next & jnp.logical_not(is_edge)

    barrier = pltpu.get_barrier_semaphore()

    def signal(seq_to):
        pl.semaphore_signal(barrier, inc=1, device_id={"seq": seq_to}, device_id_type=MESH)

    @pl.when(has_prev)
    def _():
        signal(seq - 1)

    @pl.when(has_next)
    def _():
        signal(seq + 1)

    @pl.when(is_edge | (seq == boundary))
    def _():
        signal(last)

    @pl.when(is_relay)
    def _():
        signal(boundary - 1)
        signal(boundary)

    @pl.when(jnp.logical_not(is_long))
    def _():
        def greet(r, _):
            pl.semaphore_signal(barrier, inc=1, device_id={"dp": lax.rem(dp + r, groups)}, device_id_type=MESH)
            return 0

        lax.fori_loop(1, groups, greet, 0)
        pl.semaphore_wait(barrier, groups - 1)

    three = is_edge | (seq == boundary) | is_relay

    @pl.when(three)
    def _():
        pl.semaphore_wait(barrier, 3)

    @pl.when(has_prev & has_next & jnp.logical_not(three))
    def _():
        pl.semaphore_wait(barrier, 2)

    @pl.when(is_long & jnp.logical_not(has_prev))
    def _():
        pl.semaphore_wait(barrier, 1)

    lane_token = lax.broadcasted_iota(jnp.int32, (1, tile_rows), 1) // per

    def row_mean(group):
        total = reward_ref[group, 0]
        for r in range(1, rolls):
            total = total + reward_ref[group, r]
        return total * (1.0 / rolls)

    def tile(g, i, start, token, live, weight, k, v, kt_of, vt_of, add_dk, add_dv, key0, chunk, chunks, hook):
        spot = pl.ds(pl.multiple_of(i * BLK, BLK), BLK)
        q = q_v[spot, g].astype(jnp.float32).reshape(tile_rows, DH).astype(jnp.bfloat16)
        up = up_v[spot, g].astype(jnp.float32).reshape(tile_rows, DH)
        out, dq = attend_tile(
            q, up, start, token, live, weight, k, v, kt_of, vt_of, add_dk, add_dv, s_ref, p_ref, key0, chunk, chunks, hook
        )
        o_ref[spot, g] = out.reshape(BLK, per, DH).astype(jnp.bfloat16)
        dq_ref[spot, g] = dq.reshape(BLK, per, DH).astype(jnp.bfloat16)

    up_load = pltpu.make_async_copy(up_hbm, up_v, load_sem.at[0])

    @pl.when(is_long)
    def _():
        q_load = pltpu.make_async_copy(q_hbm, q_v, load_sem.at[1])
        kv_load = pltpu.make_async_copy(kv_hbm, kw.at[:, :, pl.ds(OWN, tokens)], load_sem.at[2])
        kv_load.start()
        kv_load.wait()
        hop_from = (OWN, OWN - tokens, OWN - 2 * tokens, BLK * 2)
        hop_to = (OWN - tokens, OWN - 2 * tokens, OWN - 3 * tokens, 0)
        hop_rows = (tokens, tokens, tokens, BLK)

        def hop(src, dst, recv, seq_to, g, k):
            return pltpu.make_async_remote_copy(
                src_ref=src, dst_ref=dst, send_sem=gather_send.at[g, k], recv_sem=recv.at[g, k],
                device_id={"seq": seq_to}, device_id_type=MESH,
            )

        def gather(g, k):
            return hop(kw.at[g, :, pl.ds(hop_from[k], hop_rows[k])], kw.at[g, :, pl.ds(hop_to[k], hop_rows[k])],
                       gather_recv, seq + 1, g, k)

        def edge(g, k):
            return hop(kw.at[g, :, pl.ds(hop_from[k], hop_rows[k])], relay_v.at[g, :, pl.ds(hop_to[k], hop_rows[k])],
                       relay_recv, last, g, k)

        def relay(g, k):
            at = pl.ds(hop_to[k], hop_rows[k])
            return hop(relay_v.at[g, :, at], kw.at[g, :, at], gather_recv, boundary, g, k)

        def gather_arrived(g, k, when=True):
            @pl.when(has_prev & when)
            def _():
                gather(g, k).wait_recv()

        def gather_step(g, k, when=True):
            if k > 0:
                gather_arrived(g, k - 1, when)

            @pl.when(plain_next & when)
            def _():
                gather(g, k).start()

            @pl.when(is_edge & when)
            def _():
                edge(g, k).start()

        def relay_step(g, k, when=True):
            @pl.when(is_relay & when)
            def _():
                edge(g, k).wait_recv()
                relay(g, k).start()

        part_at = (0, BLK, 3 * BLK, 5 * BLK, 7 * BLK)
        part_rows = (BLK, tokens, tokens, tokens, tokens)

        def chain(g, k):
            return pltpu.make_async_remote_copy(
                src_ref=sbuf.at[g, k, :, pl.ds(0, part_rows[k])],
                dst_ref=rbuf.at[g, k, :, pl.ds(0, part_rows[k])],
                send_sem=chain_send.at[g, k],
                recv_sem=chain_recv.at[g, k],
                device_id={"seq": seq - 1},
                device_id_type=MESH,
            )

        def chain_step(g, k, when=True):
            if k > 0:
                @pl.when(has_next & when)
                def _():
                    chain(g, k - 1).wait_recv()
                    got = part_rows[k - 1]
                    at = pl.ds(part_at[k] + tokens - got, got)
                    dkv[g, :, at] += rbuf[g, k - 1, :, :got].astype(jnp.float32)

            if k < 4:
                @pl.when(has_prev & when)
                def _():
                    sbuf[g, k, :, : part_rows[k]] = dkv[g, :, pl.ds(part_at[k], part_rows[k])].astype(jnp.bfloat16)
                    chain(g, k).start()
            else:
                @pl.when(when)
                def _():
                    dkv_ref[g, 0] = (dkv[g, 0, pl.ds(OWN, tokens)] * SCALE).astype(jnp.bfloat16)
                    dkv_ref[g, 1] = dkv[g, 1, pl.ds(OWN, tokens)].astype(jnp.bfloat16)

        def clear_first():
            @pl.when(jnp.logical_not(has_prev))
            def _():
                kw[:, :, :OWN] = jnp.zeros((kv_count, 2, OWN, DH), kw.dtype)

        gather_step(0, 0)
        clear_first()
        q_load.start()
        up_load.start()
        dkv[...] = jnp.zeros_like(dkv)
        relay_step(0, 0)
        gather_step(0, 1)
        relay_step(0, 1)
        gather_step(0, 2)
        gather_step(1, 0)
        relay_step(0, 2)
        relay_step(1, 0)
        gather_step(0, 3)
        gather_step(1, 1)
        relay_step(0, 3)
        relay_step(1, 1)

        mean = row_mean(dp)
        first = [block_ref[dp, j] * BLK for j in range(SHORTS, rolls)]
        stop = [f + length_ref[dp, j] for f, j in zip(first, range(SHORTS, rolls))]
        gain = [reward_ref[dp, j] - mean for j in range(SHORTS, rolls)]
        base = seq * tokens - OWN

        q_load.wait()
        up_load.wait()
        gather_arrived(0, 3)

        def turn(t, _):
            g = t // here
            i = lax.rem(t, here)
            start_head, end_head = i == 0, i == here - 1
            g1, g2 = jnp.minimum(g + 1, kv_count - 1), jnp.minimum(g + 2, kv_count - 1)
            b1, b2 = jnp.maximum(g - 1, 0), jnp.maximum(g - 2, 0)
            more1, more2, done1, done2 = g < kv_count - 1, g < kv_count - 2, g > 0, g > 1

            def hook(p):
                if p == 0:
                    for n, at in enumerate((start_head, end_head)):
                        gather_step(g1, 2 + n, more1 & at)
                        gather_step(g2, n, more2 & at)
                    chain_step(b1, 1, done1 & start_head)
                    chain_step(b2, 3, done2 & start_head)
                    chain_step(g, 0, end_head)
                    chain_step(b1, 2, done1 & end_head)
                    chain_step(b2, 4, done2 & end_head)
                if p == 2:
                    for n, at in enumerate((start_head, end_head)):
                        relay_step(g1, 2 + n, more1 & at)
                        relay_step(g2, n, more2 & at)

            @pl.when(start_head)
            def _():
                kt[0] = kw[g, 0].T
                kt[1] = kw[g, 1].T

            off = pl.multiple_of(i * BLK, BLK)

            def at(c):
                return pl.ds(pl.multiple_of(off + c * CHUNK, BLK), CHUNK)

            def add(which):
                def one(c, value):
                    dkv[g, which, at(c)] += value

                return one

            token = OWN + i * BLK + lane_token
            start = jnp.full(token.shape, NEVER, jnp.int32)
            live = jnp.zeros(token.shape, jnp.float32)
            weight = jnp.zeros(token.shape, jnp.float32)
            for f, e, w in zip(first, stop, gain):
                inside = (token >= f - base) & (token < e - base)
                start = jnp.where(inside, f - base, start)
                live = jnp.where(inside, 1.0, live)
                weight = jnp.where(inside, w, weight)

            tile(g, i, start, token, live, weight,
                 lambda c: kw[g, 0, at(c)], lambda c: kw[g, 1, at(c)], lambda c: kt[0, :, at(c)], lambda c: kt[1, :, at(c)],
                 add(0), add(1), off, CHUNK, (WINDOW - BLK) // CHUNK, hook)
            gather_arrived(g1, 3, more1 & end_head)
            return 0

        lax.fori_loop(0, kv_count * here, turn, 0)
        final = kv_count - 1
        chain_step(final, 1)
        chain_step(final - 1, 3)
        chain_step(final, 2)
        chain_step(final - 1, 4)
        chain_step(final, 3)
        chain_step(final, 4)
        for g in range(kv_count):
            for k in range(4):
                @pl.when(has_next | is_relay)
                def _():
                    gather(g, k).wait_send()

                @pl.when(has_prev)
                def _():
                    chain(g, k).wait_send()

    @pl.when(jnp.logical_not(is_long))
    def _():
        r1q, s2q, r1k, s2k = (r1q0, r1q1), (s2q0, s2q1), (r1k0, r1k1), (s2k0, s2k1)
        piece = BLK // groups
        parts = groups // (2 * kv_count)
        kv_piece = BLK // parts

        def kv_spot(ref, m, i):
            head = m // (2 * parts)
            which = lax.rem(m // parts, 2)
            return ref.at[head, which, pl.ds(pl.multiple_of(i * BLK + lax.rem(m, parts) * kv_piece, kv_piece), kv_piece)]

        def q_spot(ref, m, i):
            return ref.at[pl.ds(pl.multiple_of(i * BLK + m * piece, piece), piece)]

        def remote(src, dst, n, d):
            return pltpu.make_async_remote_copy(
                src_ref=src, dst_ref=dst, send_sem=x_send.at[n], recv_sem=x_recv.at[n], device_id={"dp": d}, device_id_type=MESH
            )

        for i in range(here):
            pltpu.make_async_copy(q_spot(q_hbm, dp, i), r1q[i].at[dp], x_recv.at[4 * i]).start()
            pltpu.make_async_copy(kv_spot(kv_hbm, dp, i), r1k[i].at[dp], x_recv.at[4 * i + 1]).start()

            def spread(r, _):
                d = lax.rem(dp + r, groups)
                remote(q_spot(q_hbm, d, i), r1q[i].at[dp], 4 * i, d).start()
                remote(kv_spot(kv_hbm, d, i), r1k[i].at[dp], 4 * i + 1, d).start()
                return 0

            lax.fori_loop(1, groups, spread, 0)
        up_load.start()

        def plan(n, _):
            i = n // groups
            d = lax.rem(n, groups)
            found = jnp.int32(0)
            for s in range(groups):
                found = jnp.where(plan_ref[s, seq * here + i] == d, jnp.int32(s), found)
            source_ref[i, d] = found
            return 0

        lax.fori_loop(0, here * groups, plan, 0)

        for i in range(here):
            pltpu.make_async_copy(r1q[i], r1q[i], x_recv.at[4 * i]).wait()
            pltpu.make_async_copy(r1k[i], r1k[i], x_recv.at[4 * i + 1]).wait()

            def send_on(r, _):
                d = lax.rem(dp + r, groups)
                source = source_ref[i, d]
                s2q[i][d] = r1q[i][source]
                s2k[i][d] = r1k[i][source]
                remote(s2q[i].at[d], q_spot(q_v, dp, i), 4 * i + 2, d).start()
                remote(s2k[i].at[d], kv_spot(kw, dp, i), 4 * i + 3, d).start()
                return 0

            lax.fori_loop(1, groups, send_on, 0)
            source = source_ref[i, dp]
            q_v[pl.ds(pl.multiple_of(i * BLK + dp * piece, piece), piece)] = r1q[i][source]
            mine = dp // (2 * parts), lax.rem(dp // parts, 2), pl.multiple_of(i * BLK + lax.rem(dp, parts) * kv_piece, kv_piece)
            kw[mine[0], mine[1], pl.ds(mine[2], kv_piece)] = r1k[i][source]

        up_load.wait()
        most = pl.ds(0, groups - 1)
        for i in range(here):
            pltpu.make_async_copy(s2q[i].at[most], s2q[i].at[most], x_recv.at[4 * i + 2]).wait()
            pltpu.make_async_copy(s2k[i].at[most], s2k[i].at[most], x_recv.at[4 * i + 3]).wait()
            at = pl.ds(i * BLK, BLK)
            source = source_ref[i, dp]
            slot = seq * here + i
            gain = reward_ref[source, slot] - row_mean(source)
            inside = lane_token < length_ref[source, slot]
            live = jnp.where(inside, 1.0, 0.0)
            weight = jnp.where(inside, gain, 0.0)
            start = jnp.where(inside, 0, NEVER)

            def small(g, _):
                kt[0, :, :BLK] = kw[g, 0, at].T
                kt[1, :, :BLK] = kw[g, 1, at].T

                def keys_out(c, value):
                    dkv_ref[g, 0, at] = (value * SCALE).astype(jnp.bfloat16)

                def values_out(c, value):
                    dkv_ref[g, 1, at] = value.astype(jnp.bfloat16)

                tile(g, i, start, lane_token, live, weight,
                     lambda c: kw[g, 0, at], lambda c: kw[g, 1, at], lambda c: kt[0, :, :BLK], lambda c: kt[1, :, :BLK],
                     keys_out, values_out, 0, BLK, 1, lambda p: None)
                return 0

            lax.fori_loop(0, kv_count, small, 0)
        for i in range(here):
            for phase in range(2):
                pltpu.make_async_copy(s2q[i].at[most], s2q[i].at[most], x_send.at[4 * i + 2 * phase]).wait()
                pltpu.make_async_copy(s2k[i].at[most], s2k[i].at[most], x_send.at[4 * i + 2 * phase + 1]).wait()


def attention(q, up, kv, plans, groups, seq_count, short_rows):
    tokens, kv_count, per, _ = q.shape
    half = jnp.bfloat16
    piece = BLK // groups
    kv_piece = BLK // (groups // (2 * kv_count))
    tile_rows = BLK * per
    any_spec = pl.BlockSpec(memory_space=pl.ANY)
    vmem = pl.BlockSpec(memory_space=pltpu.VMEM)
    smem = pl.BlockSpec(memory_space=pltpu.SMEM)
    q_pieces = pltpu.VMEM((groups, piece, kv_count, per, DH), half)
    kv_pieces = pltpu.VMEM((groups, kv_piece, DH), half)
    per_hop = pltpu.SemaphoreType.DMA((kv_count, 4))
    chunks = (WINDOW - BLK) // CHUNK
    return pl.pallas_call(
        functools.partial(kernel, groups, seq_count, short_rows, seq_count // 2),
        in_specs=[any_spec, any_spec, any_spec, smem, smem, smem, smem],
        out_specs=[vmem, vmem, vmem],
        out_shape=[
            jax.ShapeDtypeStruct(q.shape, half),
            jax.ShapeDtypeStruct(q.shape, half),
            jax.ShapeDtypeStruct(kv.shape, half),
        ],
        scratch_shapes=[
            pltpu.VMEM(q.shape, half),
            pltpu.VMEM(q.shape, half),
            pltpu.VMEM((kv_count, 2, WINDOW, DH), half),
            pltpu.VMEM((kv_count, 2, OWN, DH), half),
            pltpu.VMEM((2, DH, WINDOW), half),
            pltpu.VMEM((kv_count, 2, WINDOW, DH), jnp.float32),
            pltpu.VMEM((chunks, CHUNK, tile_rows), jnp.float32),
            pltpu.VMEM((chunks, CHUNK, tile_rows), half),
            pltpu.VMEM((kv_count, 4, 2, tokens, DH), half),
            pltpu.VMEM((kv_count, 4, 2, tokens, DH), half),
            q_pieces, q_pieces, q_pieces, q_pieces,
            kv_pieces, kv_pieces, kv_pieces, kv_pieces,
            pltpu.SMEM((tokens // BLK, groups), jnp.int32),
            pltpu.SemaphoreType.DMA((3,)),
            per_hop, per_hop, per_hop, per_hop, per_hop,
            pltpu.SemaphoreType.DMA((8,)),
            pltpu.SemaphoreType.DMA((8,)),
        ],
        compiler_params=pltpu.CompilerParams(
            collective_id=0, has_side_effects=True, vmem_limit_bytes=52 * 1024 * 1024
        ),
    )(q, up, kv, *plans)


def body(queries, keys, values, upstream, rewards, response_length, block_start, move_plan):
    groups = lax.axis_size("dp")
    seq_count = lax.axis_size("seq")
    tokens, heads, _ = queries.shape
    kv_count = keys.shape[1]
    per = heads // kv_count
    short_rows = SHORTS // (tokens // BLK)
    q = queries.reshape(tokens, kv_count, per, DH)
    up = upstream.reshape(tokens, kv_count, per, DH)
    kv = jnp.stack([keys, values]).transpose(2, 0, 1, 3)
    plans = (rewards, response_length, block_start, move_plan)
    out, dq, grads = attention(q, up, kv, plans, groups, seq_count, short_rows)
    grads = grads.transpose(1, 2, 0, 3)
    return (out.reshape(queries.shape), dq.reshape(queries.shape), grads[0], grads[1])


def solution(mesh):
    spec = P(("dp", "seq"), None, None)
    return jax.shard_map(
        body,
        mesh=mesh,
        in_specs=(spec,) * 4 + (P(),) * 4,
        out_specs=(spec,) * 4,
        check_vma=False,
    )
```

time: 144 us -> 106 us (0.74); the launches traced: 142 us -> 106 us
  Pallas kernels: 131 us -> 98.2 us
  other arithmetic: 2.78 us -> 0.05 us
    pallas_call x1, Pallas kernels: 131 us -> 98.2 us  [attention(): pl.pallas_call(functools.partial(kernel, groups, seq_count, short_rows, s...]
    reduce_sum x6 -> x0, other arithmetic: 2.69 us -> none  [the longest x1 0.81 us: row_tables(): advantage = rewards - jnp.mean(rewards, axis=1, keepdims=True)]
    unnamed x8 -> x16, local copies, waits for them, and re-layouts: 5.48 us -> 5.5 us
where the time goes in v3:
time: 106 us
  Pallas kernels  98.2 us (93%)
  local copies, waits for them, and re-layouts  6.66 us (6%)
    pallas_call x1, Pallas kernels, attention(): pl.pallas_call(functools.partial(kernel, groups, seq_count, short_rows, s...  98.2 us
    unnamed x16, local copies, waits for them, and re-layouts  5.5 us

profile of v3, /device:TPU:134, one launch (start us, length us, event | category | flops | bytes accessed | tf_op | source)
XLA Modules:
  0.0 105.6 jit_solution(17025422573522160001)
XLA Ops:
  0.6 0.0 copy-start.3
  0.6 0.0 copy-start.2
  0.7 0.0 copy-start.1
  0.7 0.0 copy-start
  0.7 1.1 %copy_bitcast_fusion = (bf16[1,256,4,128]{3,1,0,2:T(8,128)(2,1)S(1)}, bf16[1,256,4,128]{3,1,0,2:T(8,128)(2,1)S(1)}) fusion(bf16[256,4,128]{2,1,0:T(4,128)(2,1)} %param.10, bf16[256,4,128]{2,1,0:T(4,128)(2,1)} %param.9), kind=kLoop, calls=%fused_computation.3 | loop fusion | bytes 1048576 | tf_op jit(solution)/shard_map/stack | solution.py:495
  1.8 0.1 maximum_bitcast_fusion.kv_hbm
  1.9 0.0 copy-done.3
  1.9 0.0 copy-done.2
  1.9 0.0 copy-done.1
  1.9 0.0 copy-done
  1.9 98.2 %shard_map.111 = (bf16[256,4,8,128]{3,2,1,0:T(8,128)(2,1)}, bf16[256,4,8,128]{3,2,1,0:T(8,128)(2,1)}, bf16[4,2,256,128]{3,2,1,0:T(8,128)(2,1)S(1)}) custom-call(bf16[256,4,8,128]{3,2,1,0:T(8,128)(2,1)} %bitcast.16, bf16[256,4,8,128]{3,2,1,0:T(8,128)(2,1)} %bitcast.17, bf16[4,2,256,128]{3,2,1,0:T(8,128)(2,1)S(1)} %maximum_bitcast_fusion.kv_hbm, ...), custom_call_target="tpu_custom_call" | custom-call | tf_op jit(solution)/shard_map/pallas_call | solution.py:452
  100.1 0.0 copy-start.5
  100.1 0.9 copy.15
  101.1 0.9 copy.14
  102.0 0.0 copy-done.5
  102.0 0.0 copy-start.4
  102.0 1.3 %copy.20 = bf16[256,32,128]{2,1,0:T(8,128)(2,1)} copy(bf16[256,32,128]{2,1,0:T(8,128)(2,1)S(1)} %bitcast.19) | data formatting | bytes 4194304
  103.3 1.0 copy-done.4
  104.3 1.3 %copy.21 = bf16[256,32,128]{2,1,0:T(8,128)(2,1)} copy(bf16[256,32,128]{2,1,0:T(8,128)(2,1)S(1)} %bitcast.18) | data formatting | bytes 4194304
  (1 shorter events, 0.0 us)
Async XLA Ops:
  0.6 1.2 %copy-start.3 = (s32[16,11]{1,0:T(8,128)S(1)}, s32[16,11]{1,0:T(8,128)}, u32[]{:S(2)}) copy-start(s32[16,11]{1,0:T(8,128)} %plan_ref.1) | copy-start | bytes 2116
  0.6 1.2 %copy-start.2 = (s32[16,11]{1,0:T(8,128)S(1)}, s32[16,11]{1,0:T(8,128)}, u32[]{:S(2)}) copy-start(s32[16,11]{1,0:T(8,128)} %block_ref.1) | copy-start | bytes 2116
  0.7 1.2 %copy-start.1 = (s32[16,11]{1,0:T(8,128)S(1)}, s32[16,11]{1,0:T(8,128)}, u32[]{:S(2)}) copy-start(s32[16,11]{1,0:T(8,128)} %length_ref.1) | copy-start | bytes 2116
  0.7 1.2 %copy-start = (f32[16,11]{1,0:T(8,128)S(1)}, f32[16,11]{1,0:T(8,128)}, u32[]{:S(2)}) copy-start(f32[16,11]{1,0:T(8,128)} %reward_ref.1) | copy-start | bytes 2116
  100.1 1.9 %copy-start.5 = (bf16[256,4,8,128]{3,2,1,0:T(8,128)(2,1)S(1)}, bf16[256,4,8,128]{3,2,1,0:T(8,128)(2,1)}, u32[]{:S(2)}) copy-start(bf16[256,4,8,128]{3,2,1,0:T(8,128)(2,1)} %get-tuple-element.7) | copy-start | bytes 6291460
  102.0 2.3 %copy-start.4 = (bf16[256,4,8,128]{3,2,1,0:T(8,128)(2,1)S(1)}, bf16[256,4,8,128]{3,2,1,0:T(8,128)(2,1)}, u32[]{:S(2)}) copy-start(bf16[256,4,8,128]{3,2,1,0:T(8,128)(2,1)} %get-tuple-element.8) | copy-start | bytes 6291460

commit v4 on v3

--- a/solution.py
+++ b/solution.py
@@ -61,11 +61,13 @@
         add_dv(c, dot(p16, scaled16, NT))
         add_dk(c, dot(ds, q, NN))
         dq_t = dq_t + dot(kt(c), ds, NN)
+        if c == 0:
+            hook(3)
     return out_t.T, (dq_t * SCALE).T
 
 
 def kernel(groups, seq_count, short_rows, boundary, q_hbm, up_hbm, kv_hbm, reward_ref, length_ref, block_ref, plan_ref,
-           o_ref, dq_ref, dkv_ref,
+           o_ref, dq_ref, dk_ref, dv_ref,
            q_v, up_v, kw, relay_v, kt, dkv, s_ref, p_ref, sbuf, rbuf,
            r1q0, r1q1, s2q0, s2q1, r1k0, r1k1, s2k0, s2k1, source_ref,
            load_sem, gather_send, gather_recv, relay_recv, chain_send, chain_recv, x_send, x_recv):
@@ -158,79 +160,86 @@
         hop_to = (OWN - tokens, OWN - 2 * tokens, OWN - 3 * tokens, 0)
         hop_rows = (tokens, tokens, tokens, BLK)
 
-        def hop(src, dst, recv, seq_to, g, k):
+        def hop(src, dst, recv, seq_to, g, k, w):
             return pltpu.make_async_remote_copy(
-                src_ref=src, dst_ref=dst, send_sem=gather_send.at[g, k], recv_sem=recv.at[g, k],
+                src_ref=src, dst_ref=dst, send_sem=gather_send.at[g, 2 * k + w], recv_sem=recv.at[g, 2 * k + w],
                 device_id={"seq": seq_to}, device_id_type=MESH,
             )
 
-        def gather(g, k):
-            return hop(kw.at[g, :, pl.ds(hop_from[k], hop_rows[k])], kw.at[g, :, pl.ds(hop_to[k], hop_rows[k])],
-                       gather_recv, seq + 1, g, k)
-
-        def edge(g, k):
-            return hop(kw.at[g, :, pl.ds(hop_from[k], hop_rows[k])], relay_v.at[g, :, pl.ds(hop_to[k], hop_rows[k])],
-                       relay_recv, last, g, k)
-
-        def relay(g, k):
+        def gather(g, k, w):
+            return hop(kw.at[g, w, pl.ds(hop_from[k], hop_rows[k])], kw.at[g, w, pl.ds(hop_to[k], hop_rows[k])],
+                       gather_recv, seq + 1, g, k, w)
+
+        def edge(g, k, w):
+            return hop(kw.at[g, w, pl.ds(hop_from[k], hop_rows[k])], relay_v.at[g, w, pl.ds(hop_to[k], hop_rows[k])],
+                       relay_recv, last, g, k, w)
+
+        def relay(g, k, w):
             at = pl.ds(hop_to[k], hop_rows[k])
-            return hop(relay_v.at[g, :, at], kw.at[g, :, at], gather_recv, boundary, g, k)
-
-        def gather_arrived(g, k, when=True):
+            return hop(relay_v.at[g, w, at], kw.at[g, w, at], gather_recv, boundary, g, k, w)
+
+        def gather_arrived(g, k, w, when=True):
             @pl.when(has_prev & when)
             def _():
-                gather(g, k).wait_recv()
+                gather(g, k, w).wait_recv()
 
         def gather_step(g, k, when=True):
-            if k > 0:
-                gather_arrived(g, k - 1, when)
-
-            @pl.when(plain_next & when)
-            def _():
-                gather(g, k).start()
-
-            @pl.when(is_edge & when)
-            def _():
-                edge(g, k).start()
+            for w in range(2):
+                if k > 0:
+                    gather_arrived(g, k - 1, w, when)
+
+                @pl.when(plain_next & when)
+                def _():
+                    gather(g, k, w).start()
+
+                @pl.when(is_edge & when)
+                def _():
+                    edge(g, k, w).start()
 
         def relay_step(g, k, when=True):
             @pl.when(is_relay & when)
             def _():
-                edge(g, k).wait_recv()
-                relay(g, k).start()
+                for w in range(2):
+                    edge(g, k, w).wait_recv()
+                    relay(g, k, w).start()
 
         part_at = (0, BLK, 3 * BLK, 5 * BLK, 7 * BLK)
         part_rows = (BLK, tokens, tokens, tokens, tokens)
 
-        def chain(g, k):
+        def chain(g, k, w):
             return pltpu.make_async_remote_copy(
-                src_ref=sbuf.at[g, k, :, pl.ds(0, part_rows[k])],
-                dst_ref=rbuf.at[g, k, :, pl.ds(0, part_rows[k])],
-                send_sem=chain_send.at[g, k],
-                recv_sem=chain_recv.at[g, k],
+                src_ref=sbuf.at[g, k, w, pl.ds(0, part_rows[k])],
+                dst_ref=rbuf.at[g, k, w, pl.ds(0, part_rows[k])],
+                send_sem=chain_send.at[g, 2 * k + w],
+                recv_sem=chain_recv.at[g, 2 * k + w],
                 device_id={"seq": seq - 1},
                 device_id_type=MESH,
             )
 
         def chain_step(g, k, when=True):
-            if k > 0:
-                @pl.when(has_next & when)
-                def _():
-                    chain(g, k - 1).wait_recv()
-                    got = part_rows[k - 1]
-                    at = pl.ds(part_at[k] + tokens - got, got)
-                    dkv[g, :, at] += rbuf[g, k - 1, :, :got].astype(jnp.float32)
-
-            if k < 4:
-                @pl.when(has_prev & when)
-                def _():
-                    sbuf[g, k, :, : part_rows[k]] = dkv[g, :, pl.ds(part_at[k], part_rows[k])].astype(jnp.bfloat16)
-                    chain(g, k).start()
-            else:
-                @pl.when(when)
-                def _():
-                    dkv_ref[g, 0] = (dkv[g, 0, pl.ds(OWN, tokens)] * SCALE).astype(jnp.bfloat16)
-                    dkv_ref[g, 1] = dkv[g, 1, pl.ds(OWN, tokens)].astype(jnp.bfloat16)
+            for w in range(2):
+                if k > 0:
+                    @pl.when(has_next & when)
+                    def _():
+                        chain(g, k - 1, w).wait_recv()
+                        got = part_rows[k - 1]
+                        at = pl.ds(part_at[k] + tokens - got, got)
+                        dkv[g, w, at] += rbuf[g, k - 1, w, :got].astype(jnp.float32)
+
+                if k < 4:
+                    @pl.when(has_prev & when)
+                    def _():
+                        sbuf[g, k, w, : part_rows[k]] = dkv[g, w, pl.ds(part_at[k], part_rows[k])].astype(jnp.bfloat16)
+                        chain(g, k, w).start()
+                else:
+                    @pl.when(when)
+                    def _():
+                        lanes = pl.ds(pl.multiple_of(g * DH, DH), DH)
+                        total = dkv[g, w, pl.ds(OWN, tokens)]
+                        if w == 0:
+                            dk_ref[:, lanes] = (total * SCALE).astype(jnp.bfloat16)
+                        else:
+                            dv_ref[:, lanes] = total.astype(jnp.bfloat16)
 
         def clear_first():
             @pl.when(jnp.logical_not(has_prev))
@@ -262,7 +271,8 @@
 
         q_load.wait()
         up_load.wait()
-        gather_arrived(0, 3)
+        gather_arrived(0, 3, 0)
+        gather_arrived(0, 3, 1)
 
         def turn(t, _):
             g = t // here
@@ -276,16 +286,20 @@
                 if p == 0:
                     for n, at in enumerate((start_head, end_head)):
                         gather_step(g1, 2 + n, more1 & at)
+                    relay_step(g2, 0, more2 & end_head)
+                    chain_step(b2, 4, done2 & start_head)
+                    chain_step(g, 0, end_head)
+                if p == 1:
+                    for n, at in enumerate((start_head, end_head)):
                         gather_step(g2, n, more2 & at)
-                    chain_step(b1, 1, done1 & start_head)
-                    chain_step(b2, 3, done2 & start_head)
-                    chain_step(g, 0, end_head)
-                    chain_step(b1, 2, done1 & end_head)
-                    chain_step(b2, 4, done2 & end_head)
+                    chain_step(b1, 2, done1 & start_head)
+                    chain_step(b1, 3, done1 & end_head)
                 if p == 2:
                     for n, at in enumerate((start_head, end_head)):
                         relay_step(g1, 2 + n, more1 & at)
-                        relay_step(g2, n, more2 & at)
+                if p == 3:
+                    relay_step(g2, 1, more2 & end_head)
+                    chain_step(g, 1, end_head)
 
             @pl.when(start_head)
             def _():
@@ -316,26 +330,26 @@
             tile(g, i, start, token, live, weight,
                  lambda c: kw[g, 0, at(c)], lambda c: kw[g, 1, at(c)], lambda c: kt[0, :, at(c)], lambda c: kt[1, :, at(c)],
                  add(0), add(1), off, CHUNK, (WINDOW - BLK) // CHUNK, hook)
-            gather_arrived(g1, 3, more1 & end_head)
+            gather_arrived(g1, 3, 0, more1 & end_head)
+            gather_arrived(g1, 3, 1, more1 & end_head)
             return 0
 
         lax.fori_loop(0, kv_count * here, turn, 0)
         final = kv_count - 1
-        chain_step(final, 1)
-        chain_step(final - 1, 3)
         chain_step(final, 2)
         chain_step(final - 1, 4)
         chain_step(final, 3)
         chain_step(final, 4)
         for g in range(kv_count):
             for k in range(4):
-                @pl.when(has_next | is_relay)
-                def _():
-                    gather(g, k).wait_send()
-
-                @pl.when(has_prev)
-                def _():
-                    chain(g, k).wait_send()
+                for w in range(2):
+                    @pl.when(has_next | is_relay)
+                    def _():
+                        gather(g, k, w).wait_send()
+
+                    @pl.when(has_prev)
+                    def _():
+                        chain(g, k, w).wait_send()
 
     @pl.when(jnp.logical_not(is_long))
     def _():
@@ -417,12 +431,13 @@
             def small(g, _):
                 kt[0, :, :BLK] = kw[g, 0, at].T
                 kt[1, :, :BLK] = kw[g, 1, at].T
+                lanes = pl.ds(pl.multiple_of(g * DH, DH), DH)
 
                 def keys_out(c, value):
-                    dkv_ref[g, 0, at] = (value * SCALE).astype(jnp.bfloat16)
+                    dk_ref[at, lanes] = (value * SCALE).astype(jnp.bfloat16)
 
                 def values_out(c, value):
-                    dkv_ref[g, 1, at] = value.astype(jnp.bfloat16)
+                    dv_ref[at, lanes] = value.astype(jnp.bfloat16)
 
                 tile(g, i, start, lane_token, live, weight,
                      lambda c: kw[g, 0, at], lambda c: kw[g, 1, at], lambda c: kt[0, :, :BLK], lambda c: kt[1, :, :BLK],
@@ -447,16 +462,17 @@
     smem = pl.BlockSpec(memory_space=pltpu.SMEM)
     q_pieces = pltpu.VMEM((groups, piece, kv_count, per, DH), half)
     kv_pieces = pltpu.VMEM((groups, kv_piece, DH), half)
-    per_hop = pltpu.SemaphoreType.DMA((kv_count, 4))
+    per_hop = pltpu.SemaphoreType.DMA((kv_count, 8))
     chunks = (WINDOW - BLK) // CHUNK
     return pl.pallas_call(
         functools.partial(kernel, groups, seq_count, short_rows, seq_count // 2),
         in_specs=[any_spec, any_spec, any_spec, smem, smem, smem, smem],
-        out_specs=[vmem, vmem, vmem],
+        out_specs=[vmem, vmem, vmem, vmem],
         out_shape=[
             jax.ShapeDtypeStruct(q.shape, half),
             jax.ShapeDtypeStruct(q.shape, half),
-            jax.ShapeDtypeStruct(kv.shape, half),
+            jax.ShapeDtypeStruct((tokens, kv_count * DH), half),
+            jax.ShapeDtypeStruct((tokens, kv_count * DH), half),
         ],
         scratch_shapes=[
             pltpu.VMEM(q.shape, half),
@@ -494,9 +510,8 @@
     up = upstream.reshape(tokens, kv_count, per, DH)
     kv = jnp.stack([keys, values]).transpose(2, 0, 1, 3)
     plans = (rewards, response_length, block_start, move_plan)
-    out, dq, grads = attention(q, up, kv, plans, groups, seq_count, short_rows)
-    grads = grads.transpose(1, 2, 0, 3)
-    return (out.reshape(queries.shape), dq.reshape(queries.shape), grads[0], grads[1])
+    out, dq, dk, dv = attention(q, up, kv, plans, groups, seq_count, short_rows)
+    return (out.reshape(queries.shape), dq.reshape(queries.shape), dk.reshape(keys.shape), dv.reshape(values.shape))
 
 
 def solution(mesh):

time: 106 us -> 106 us (level); the launches traced: 106 us -> 105 us
  Pallas kernels: 98.2 us -> 96.4 us
    pallas_call x1, Pallas kernels: 98.2 us -> 96.4 us  [attention(): pl.pallas_call(functools.partial(kernel, groups, seq_count, short_rows, s...]
    reshape x0 -> x2, local copies, waits for them, and re-layouts: none -> 1.53 us  [the longest x1 0.77 us: body(): dk.reshape(keys.shape)]
    unnamed x16 -> x12, local copies, waits for them, and re-layouts: 5.5 us -> 4.76 us
where the time goes in v4:
time: 106 us; the launch traced here: 105 us
  Pallas kernels  96.4 us (91%)
  local copies, waits for them, and re-layouts  7.41 us (7%)
    pallas_call x1, Pallas kernels, attention(): pl.pallas_call(functools.partial(kernel, groups, seq_count, short_rows, s...  96.4 us
    unnamed x12, local copies, waits for them, and re-layouts  4.76 us

profile of v4, /device:TPU:134, one launch (start us, length us, event | category | flops | bytes accessed | tf_op | source)
XLA Modules:
  0.0 104.5 jit_solution(13269131284092101403)
XLA Ops:
  0.6 0.0 copy-start.3
  0.6 0.0 copy-start.2
  0.7 0.0 copy-start.1
  0.7 0.0 copy-start
  0.7 1.1 %copy_bitcast_fusion = (bf16[1,256,4,128]{3,1,0,2:T(8,128)(2,1)S(1)}, bf16[1,256,4,128]{3,1,0,2:T(8,128)(2,1)S(1)}) fusion(bf16[256,4,128]{2,1,0:T(4,128)(2,1)} %param.10, bf16[256,4,128]{2,1,0:T(4,128)(2,1)} %param.9), kind=kLoop, calls=%fused_computation.1 | loop fusion | bytes 1048576 | tf_op jit(solution)/shard_map/stack | solution.py:511
  1.8 0.1 maximum_bitcast_fusion.kv_hbm
  1.9 0.0 copy-done.3
  1.9 0.0 copy-done.2
  1.9 0.0 copy-done.1
  1.9 0.0 copy-done
  1.9 96.4 %shard_map.111 = (bf16[256,4,8,128]{3,2,1,0:T(8,128)(2,1)}, bf16[256,4,8,128]{3,2,1,0:T(8,128)(2,1)}, bf16[256,512]{1,0:T(8,128)(2,1)S(1)}, bf16[256,512]{1,0:T(8,128)(2,1)S(1)}) custom-call(bf16[256,4,8,128]{3,2,1,0:T(8,128)(2,1)} %bitcast.10, bf16[256,4,8,128]{3,2,1,0:T(8,128)(2,1)} %bitcast.11, bf16[4,2,256,128]{3,2,1,0:T(8,128)(2,1)S(1)} %maximum_bitcast_fusion.kv_hbm, ...), custom_call_target="tpu_custom_call" | custom-call | tf_op jit(solution)/shard_map/pallas_call | solution.py:467
  98.3 0.8 reshape.30
  99.0 0.8 reshape.31
  99.8 0.0 copy-start.4
  99.8 3.4 %copy.18 = bf16[256,32,128]{2,1,0:T(8,128)(2,1)} copy(bf16[256,32,128]{2,1,0:T(8,128)(2,1)} %bitcast.13) | data formatting | bytes 4194304
  103.2 0.0 copy-done.4
  103.2 1.3 %copy.19 = bf16[256,32,128]{2,1,0:T(8,128)(2,1)} copy(bf16[256,32,128]{2,1,0:T(8,128)(2,1)S(1)} %bitcast.12) | data formatting | bytes 4194304
Async XLA Ops:
  0.6 1.2 %copy-start.3 = (s32[16,11]{1,0:T(8,128)S(1)}, s32[16,11]{1,0:T(8,128)}, u32[]{:S(2)}) copy-start(s32[16,11]{1,0:T(8,128)} %plan_ref.1) | copy-start | bytes 2116
  0.6 1.2 %copy-start.2 = (s32[16,11]{1,0:T(8,128)S(1)}, s32[16,11]{1,0:T(8,128)}, u32[]{:S(2)}) copy-start(s32[16,11]{1,0:T(8,128)} %block_ref.1) | copy-start | bytes 2116
  0.7 1.2 %copy-start.1 = (s32[16,11]{1,0:T(8,128)S(1)}, s32[16,11]{1,0:T(8,128)}, u32[]{:S(2)}) copy-start(s32[16,11]{1,0:T(8,128)} %length_ref.1) | copy-start | bytes 2116
  0.7 1.2 %copy-start = (f32[16,11]{1,0:T(8,128)S(1)}, f32[16,11]{1,0:T(8,128)}, u32[]{:S(2)}) copy-start(f32[16,11]{1,0:T(8,128)} %reward_ref.1) | copy-start | bytes 2116
  99.8 3.4 %copy-start.4 = (bf16[256,4,8,128]{3,2,1,0:T(8,128)(2,1)S(1)}, bf16[256,4,8,128]{3,2,1,0:T(8,128)(2,1)}, u32[]{:S(2)}) copy-start(bf16[256,4,8,128]{3,2,1,0:T(8,128)(2,1)} %get-tuple-element.9) | copy-start | bytes 6291460

commit v5 on v4

--- a/solution.py
+++ b/solution.py
@@ -70,7 +70,7 @@
            o_ref, dq_ref, dk_ref, dv_ref,
            q_v, up_v, kw, relay_v, kt, dkv, s_ref, p_ref, sbuf, rbuf,
            r1q0, r1q1, s2q0, s2q1, r1k0, r1k1, s2k0, s2k1, source_ref,
-           load_sem, gather_send, gather_recv, relay_recv, chain_send, chain_recv, x_send, x_recv):
+           load_sem, gather_send, gather_recv, relay_send, relay_recv, chain_send, chain_recv, x_send, x_recv):
     seq = lax.axis_index("seq")
     dp = lax.axis_index("dp")
     tokens, kv_count, per, _ = q_v.shape
@@ -82,7 +82,8 @@
     has_prev = seq > short_rows
     has_next = is_long & (seq < last)
     is_edge = seq == boundary - 1
-    is_relay = seq == last
+    is_relay = seq == boundary
+    twin = dp + 2 - 4 * lax.rem(dp // 2, 2)
     plain_next = has_next & jnp.logical_not(is_edge)
 
     barrier = pltpu.get_barrier_semaphore()
@@ -98,14 +99,17 @@
     def _():
         signal(seq + 1)
 
-    @pl.when(is_edge | (seq == boundary))
-    def _():
-        signal(last)
+    def signal_twin(seq_to):
+        pl.semaphore_signal(barrier, inc=1, device_id={"dp": twin, "seq": seq_to}, device_id_type=MESH)
+
+    @pl.when(is_edge)
+    def _():
+        signal_twin(boundary)
 
     @pl.when(is_relay)
     def _():
-        signal(boundary - 1)
-        signal(boundary)
+        signal_twin(boundary - 1)
+        signal_twin(boundary)
 
     @pl.when(jnp.logical_not(is_long))
     def _():
@@ -116,17 +120,19 @@
         lax.fori_loop(1, groups, greet, 0)
         pl.semaphore_wait(barrier, groups - 1)
 
-    three = is_edge | (seq == boundary) | is_relay
-
-    @pl.when(three)
+    @pl.when(is_relay)
+    def _():
+        pl.semaphore_wait(barrier, 4)
+
+    @pl.when(is_edge)
     def _():
         pl.semaphore_wait(barrier, 3)
 
-    @pl.when(has_prev & has_next & jnp.logical_not(three))
+    @pl.when(has_prev & has_next & jnp.logical_not(is_edge | is_relay))
     def _():
         pl.semaphore_wait(barrier, 2)
 
-    @pl.when(is_long & jnp.logical_not(has_prev))
+    @pl.when(has_prev != has_next)
     def _():
         pl.semaphore_wait(barrier, 1)
 
@@ -160,23 +166,23 @@
         hop_to = (OWN - tokens, OWN - 2 * tokens, OWN - 3 * tokens, 0)
         hop_rows = (tokens, tokens, tokens, BLK)
 
-        def hop(src, dst, recv, seq_to, g, k, w):
+        def hop(src, dst, send, recv, device, g, k, w):
             return pltpu.make_async_remote_copy(
-                src_ref=src, dst_ref=dst, send_sem=gather_send.at[g, 2 * k + w], recv_sem=recv.at[g, 2 * k + w],
-                device_id={"seq": seq_to}, device_id_type=MESH,
+                src_ref=src, dst_ref=dst, send_sem=send.at[g, 2 * k + w], recv_sem=recv.at[g, 2 * k + w],
+                device_id=device, device_id_type=MESH,
             )
 
         def gather(g, k, w):
             return hop(kw.at[g, w, pl.ds(hop_from[k], hop_rows[k])], kw.at[g, w, pl.ds(hop_to[k], hop_rows[k])],
-                       gather_recv, seq + 1, g, k, w)
+                       gather_send, gather_recv, {"seq": seq + 1}, g, k, w)
 
         def edge(g, k, w):
             return hop(kw.at[g, w, pl.ds(hop_from[k], hop_rows[k])], relay_v.at[g, w, pl.ds(hop_to[k], hop_rows[k])],
-                       relay_recv, last, g, k, w)
+                       gather_send, relay_recv, {"dp": twin, "seq": boundary}, g, k, w)
 
         def relay(g, k, w):
             at = pl.ds(hop_to[k], hop_rows[k])
-            return hop(relay_v.at[g, w, at], kw.at[g, w, at], gather_recv, boundary, g, k, w)
+            return hop(relay_v.at[g, w, at], kw.at[g, w, at], relay_send, gather_recv, {"dp": twin, "seq": boundary}, g, k, w)
 
         def gather_arrived(g, k, w, when=True):
             @pl.when(has_prev & when)
@@ -234,12 +240,11 @@
                 else:
                     @pl.when(when)
                     def _():
-                        lanes = pl.ds(pl.multiple_of(g * DH, DH), DH)
                         total = dkv[g, w, pl.ds(OWN, tokens)]
                         if w == 0:
-                            dk_ref[:, lanes] = (total * SCALE).astype(jnp.bfloat16)
+                            dk_ref[:, pl.ds(g, 1)] = (total * SCALE)[:, None]
                         else:
-                            dv_ref[:, lanes] = total.astype(jnp.bfloat16)
+                            dv_ref[:, pl.ds(g, 1)] = total[:, None]
 
         def clear_first():
             @pl.when(jnp.logical_not(has_prev))
@@ -343,9 +348,13 @@
         for g in range(kv_count):
             for k in range(4):
                 for w in range(2):
-                    @pl.when(has_next | is_relay)
+                    @pl.when(has_next)
                     def _():
                         gather(g, k, w).wait_send()
+
+                    @pl.when(is_relay)
+                    def _():
+                        relay(g, k, w).wait_send()
 
                     @pl.when(has_prev)
                     def _():
@@ -431,13 +440,12 @@
             def small(g, _):
                 kt[0, :, :BLK] = kw[g, 0, at].T
                 kt[1, :, :BLK] = kw[g, 1, at].T
-                lanes = pl.ds(pl.multiple_of(g * DH, DH), DH)
 
                 def keys_out(c, value):
-                    dk_ref[at, lanes] = (value * SCALE).astype(jnp.bfloat16)
+                    dk_ref[at, pl.ds(g, 1)] = (value * SCALE)[:, None]
 
                 def values_out(c, value):
-                    dv_ref[at, lanes] = value.astype(jnp.bfloat16)
+                    dv_ref[at, pl.ds(g, 1)] = value[:, None]
 
                 tile(g, i, start, lane_token, live, weight,
                      lambda c: kw[g, 0, at], lambda c: kw[g, 1, at], lambda c: kt[0, :, :BLK], lambda c: kt[1, :, :BLK],
@@ -471,8 +479,8 @@
         out_shape=[
             jax.ShapeDtypeStruct(q.shape, half),
             jax.ShapeDtypeStruct(q.shape, half),
-            jax.ShapeDtypeStruct((tokens, kv_count * DH), half),
-            jax.ShapeDtypeStruct((tokens, kv_count * DH), half),
+            jax.ShapeDtypeStruct((tokens, kv_count, DH), jnp.float32),
+            jax.ShapeDtypeStruct((tokens, kv_count, DH), jnp.float32),
         ],
         scratch_shapes=[
             pltpu.VMEM(q.shape, half),
@@ -489,7 +497,7 @@
             kv_pieces, kv_pieces, kv_pieces, kv_pieces,
             pltpu.SMEM((tokens // BLK, groups), jnp.int32),
             pltpu.SemaphoreType.DMA((3,)),
-            per_hop, per_hop, per_hop, per_hop, per_hop,
+            per_hop, per_hop, per_hop, per_hop, per_hop, per_hop,
             pltpu.SemaphoreType.DMA((8,)),
             pltpu.SemaphoreType.DMA((8,)),
         ],
@@ -511,7 +519,7 @@
     kv = jnp.stack([keys, values]).transpose(2, 0, 1, 3)
     plans = (rewards, response_length, block_start, move_plan)
     out, dq, dk, dv = attention(q, up, kv, plans, groups, seq_count, short_rows)
-    return (out.reshape(queries.shape), dq.reshape(queries.shape), dk.reshape(keys.shape), dv.reshape(values.shape))
+    return (out.reshape(queries.shape), dq.reshape(queries.shape), dk.astype(keys.dtype), dv.astype(values.dtype))
 
 
 def solution(mesh):

time: 106 us -> 110 us (1.038); the launches traced: 105 us -> 110 us
  Pallas kernels: 96.4 us -> 102 us
  other arithmetic: 0.05 us -> 1.64 us
  local copies, waits for them, and re-layouts: 7.41 us -> 5.88 us
    pallas_call x1, Pallas kernels: 96.4 us -> 102 us  [attention(): pl.pallas_call(functools.partial(kernel, groups, seq_count, short_rows, s...]
    convert_element_type x0 -> x2, other arithmetic: none -> 1.59 us  [the longest x1 0.79 us: body(): dk.astype(keys.dtype)]
    reshape x2 -> x0, local copies, waits for them, and re-layouts: 1.53 us -> none  [the longest x1 0.77 us: body(): dk.reshape(keys.shape)]
where the time goes in v5:
time: 110 us
  Pallas kernels  102 us (93%)
  local copies, waits for them, and re-layouts  5.88 us (5%)
  other arithmetic  1.64 us (1%)
    pallas_call x1, Pallas kernels, attention(): pl.pallas_call(functools.partial(kernel, groups, seq_count, short_rows, s...  102 us
    unnamed x12, local copies, waits for them, and re-layouts  4.76 us

profile of v5, /device:TPU:134, one launch (start us, length us, event | category | flops | bytes accessed | tf_op | source)
XLA Modules:
  0.0 110.4 jit_solution(18392039285406610778)
XLA Ops:
  0.6 0.0 copy-start.3
  0.6 0.0 copy-start.2
  0.7 0.0 copy-start.1
  0.7 0.0 copy-start
  0.7 1.1 %copy_bitcast_fusion = (bf16[1,256,4,128]{3,1,0,2:T(8,128)(2,1)S(1)}, bf16[1,256,4,128]{3,1,0,2:T(8,128)(2,1)S(1)}) fusion(bf16[256,4,128]{2,1,0:T(4,128)(2,1)} %param.10, bf16[256,4,128]{2,1,0:T(4,128)(2,1)} %param.9), kind=kLoop, calls=%fused_computation.1 | loop fusion | bytes 1048576 | tf_op jit(solution)/shard_map/stack | solution.py:519
  1.8 0.1 maximum_bitcast_fusion.kv_hbm
  1.9 0.0 copy-done.3
  1.9 0.0 copy-done.2
  1.9 0.0 copy-done.1
  1.9 0.0 copy-done
  1.9 102.1 %shard_map.111 = (bf16[256,4,8,128]{3,2,1,0:T(8,128)(2,1)}, bf16[256,4,8,128]{3,2,1,0:T(8,128)(2,1)}, f32[256,4,128]{2,1,0:T(4,128)S(1)}, f32[256,4,128]{2,1,0:T(4,128)S(1)}) custom-call(bf16[256,4,8,128]{3,2,1,0:T(8,128)(2,1)} %bitcast.10, bf16[256,4,8,128]{3,2,1,0:T(8,128)(2,1)} %bitcast.11, bf16[4,2,256,128]{3,2,1,0:T(8,128)(2,1)S(1)} %maximum_bitcast_fusion.kv_hbm, ...), custom_call_target="tpu_custom_call" | custom-call | tf_op jit(solution)/shard_map/pallas_call | solution.py:475
  104.0 0.8 convert_element_type.6
  104.8 0.8 convert_element_type.7
  105.6 0.0 copy-start.4
  105.6 3.4 %copy.18 = bf16[256,32,128]{2,1,0:T(8,128)(2,1)} copy(bf16[256,32,128]{2,1,0:T(8,128)(2,1)} %bitcast.13) | data formatting | bytes 4194304
  109.0 0.0 copy-done.4
  109.0 1.3 %copy.19 = bf16[256,32,128]{2,1,0:T(8,128)(2,1)} copy(bf16[256,32,128]{2,1,0:T(8,128)(2,1)S(1)} %bitcast.12) | data formatting | bytes 4194304
Async XLA Ops:
  0.6 1.2 %copy-start.3 = (s32[16,11]{1,0:T(8,128)S(1)}, s32[16,11]{1,0:T(8,128)}, u32[]{:S(2)}) copy-start(s32[16,11]{1,0:T(8,128)} %plan_ref.1) | copy-start | bytes 2116
  0.6 1.2 %copy-start.2 = (s32[16,11]{1,0:T(8,128)S(1)}, s32[16,11]{1,0:T(8,128)}, u32[]{:S(2)}) copy-start(s32[16,11]{1,0:T(8,128)} %block_ref.1) | copy-start | bytes 2116
  0.7 1.2 %copy-start.1 = (s32[16,11]{1,0:T(8,128)S(1)}, s32[16,11]{1,0:T(8,128)}, u32[]{:S(2)}) copy-start(s32[16,11]{1,0:T(8,128)} %length_ref.1) | copy-start | bytes 2116
  0.7 1.2 %copy-start = (f32[16,11]{1,0:T(8,128)S(1)}, f32[16,11]{1,0:T(8,128)}, u32[]{:S(2)}) copy-start(f32[16,11]{1,0:T(8,128)} %reward_ref.1) | copy-start | bytes 2116
  105.6 3.4 %copy-start.4 = (bf16[256,4,8,128]{3,2,1,0:T(8,128)(2,1)S(1)}, bf16[256,4,8,128]{3,2,1,0:T(8,128)(2,1)}, u32[]{:S(2)}) copy-start(bf16[256,4,8,128]{3,2,1,0:T(8,128)(2,1)} %get-tuple-element.9) | copy-start | bytes 6291460

commit v6 on v5

--- a/solution.py
+++ b/solution.py
@@ -67,7 +67,7 @@
 
 
 def kernel(groups, seq_count, short_rows, boundary, q_hbm, up_hbm, kv_hbm, reward_ref, length_ref, block_ref, plan_ref,
-           o_ref, dq_ref, dk_ref, dv_ref,
+           o_ref, dq_ref, dkv_ref,
            q_v, up_v, kw, relay_v, kt, dkv, s_ref, p_ref, sbuf, rbuf,
            r1q0, r1q1, s2q0, s2q1, r1k0, r1k1, s2k0, s2k1, source_ref,
            load_sem, gather_send, gather_recv, relay_send, relay_recv, chain_send, chain_recv, x_send, x_recv):
@@ -242,9 +242,9 @@
                     def _():
                         total = dkv[g, w, pl.ds(OWN, tokens)]
                         if w == 0:
-                            dk_ref[:, pl.ds(g, 1)] = (total * SCALE)[:, None]
+                            dkv_ref[g, 0] = (total * SCALE).astype(jnp.bfloat16)
                         else:
-                            dv_ref[:, pl.ds(g, 1)] = total[:, None]
+                            dkv_ref[g, 1] = total.astype(jnp.bfloat16)
 
         def clear_first():
             @pl.when(jnp.logical_not(has_prev))
@@ -291,19 +291,16 @@
                 if p == 0:
                     for n, at in enumerate((start_head, end_head)):
                         gather_step(g1, 2 + n, more1 & at)
-                    relay_step(g2, 0, more2 & end_head)
+                        relay_step(g1, 2 + n, more1 & at)
                     chain_step(b2, 4, done2 & start_head)
                     chain_step(g, 0, end_head)
                 if p == 1:
                     for n, at in enumerate((start_head, end_head)):
                         gather_step(g2, n, more2 & at)
+                        relay_step(g2, n, more2 & at)
                     chain_step(b1, 2, done1 & start_head)
                     chain_step(b1, 3, done1 & end_head)
-                if p == 2:
-                    for n, at in enumerate((start_head, end_head)):
-                        relay_step(g1, 2 + n, more1 & at)
                 if p == 3:
-                    relay_step(g2, 1, more2 & end_head)
                     chain_step(g, 1, end_head)
 
             @pl.when(start_head)
@@ -442,10 +439,10 @@
                 kt[1, :, :BLK] = kw[g, 1, at].T
 
                 def keys_out(c, value):
-                    dk_ref[at, pl.ds(g, 1)] = (value * SCALE)[:, None]
+                    dkv_ref[g, 0, at] = (value * SCALE).astype(jnp.bfloat16)
 
                 def values_out(c, value):
-                    dv_ref[at, pl.ds(g, 1)] = value[:, None]
+                    dkv_ref[g, 1, at] = value.astype(jnp.bfloat16)
 
                 tile(g, i, start, lane_token, live, weight,
                      lambda c: kw[g, 0, at], lambda c: kw[g, 1, at], lambda c: kt[0, :, :BLK], lambda c: kt[1, :, :BLK],
@@ -475,12 +472,11 @@
     return pl.pallas_call(
         functools.partial(kernel, groups, seq_count, short_rows, seq_count // 2),
         in_specs=[any_spec, any_spec, any_spec, smem, smem, smem, smem],
-        out_specs=[vmem, vmem, vmem, vmem],
+        out_specs=[vmem, vmem, vmem],
         out_shape=[
             jax.ShapeDtypeStruct(q.shape, half),
             jax.ShapeDtypeStruct(q.shape, half),
-            jax.ShapeDtypeStruct((tokens, kv_count, DH), jnp.float32),
-            jax.ShapeDtypeStruct((tokens, kv_count, DH), jnp.float32),
+            jax.ShapeDtypeStruct(kv.shape, half),
         ],
         scratch_shapes=[
             pltpu.VMEM(q.shape, half),
@@ -518,8 +514,9 @@
     up = upstream.reshape(tokens, kv_count, per, DH)
     kv = jnp.stack([keys, values]).transpose(2, 0, 1, 3)
     plans = (rewards, response_length, block_start, move_plan)
-    out, dq, dk, dv = attention(q, up, kv, plans, groups, seq_count, short_rows)
-    return (out.reshape(queries.shape), dq.reshape(queries.shape), dk.astype(keys.dtype), dv.astype(values.dtype))
+    out, dq, grads = attention(q, up, kv, plans, groups, seq_count, short_rows)
+    grads = grads.transpose(1, 2, 0, 3)
+    return (out.reshape(queries.shape), dq.reshape(queries.shape), grads[0], grads[1])
 
 
 def solution(mesh):

time: 110 us -> 113 us (1.027)
  Pallas kernels: 102 us -> 105 us
  other arithmetic: 1.64 us -> 0.05 us
    pallas_call x1, Pallas kernels: 102 us -> 105 us  [attention(): pl.pallas_call(functools.partial(kernel, groups, seq_count, short_rows, s...]
    convert_element_type x2 -> x0, other arithmetic: 1.59 us -> none  [the longest x1 0.79 us: body(): dk.astype(keys.dtype)]
    unnamed x12 -> x16, local copies, waits for them, and re-layouts: 4.76 us -> 5.5 us
where the time goes in v6:
time: 113 us; the launch traced here: 112 us
  Pallas kernels  105 us (93%)
  local copies, waits for them, and re-layouts  6.66 us (6%)
    pallas_call x1, Pallas kernels, attention(): pl.pallas_call(functools.partial(kernel, groups, seq_count, short_rows, s...  105 us
    unnamed x16, local copies, waits for them, and re-layouts  5.5 us

profile of v6, /device:TPU:134, one launch (start us, length us, event | category | flops | bytes accessed | tf_op | source)
XLA Modules:
  0.0 112.5 jit_solution(4590122581887803627)
XLA Ops:
  0.6 0.0 copy-start.3
  0.6 0.0 copy-start.2
  0.7 0.0 copy-start.1
  0.7 0.0 copy-start
  0.7 1.1 copy_bitcast_fusion
  1.8 0.1 maximum_bitcast_fusion.kv_hbm
  1.9 0.0 copy-done.3
  1.9 0.0 copy-done.2
  1.9 0.0 copy-done.1
  1.9 0.0 copy-done
  1.9 105.0 %shard_map.111 = (bf16[256,4,8,128]{3,2,1,0:T(8,128)(2,1)}, bf16[256,4,8,128]{3,2,1,0:T(8,128)(2,1)}, bf16[4,2,256,128]{3,2,1,0:T(8,128)(2,1)S(1)}) custom-call(bf16[256,4,8,128]{3,2,1,0:T(8,128)(2,1)} %bitcast.16, bf16[256,4,8,128]{3,2,1,0:T(8,128)(2,1)} %bitcast.17, bf16[4,2,256,128]{3,2,1,0:T(8,128)(2,1)S(1)} %maximum_bitcast_fusion.kv_hbm, ...), custom_call_target="tpu_custom_call" | custom-call | tf_op jit(solution)/shard_map/pallas_call | solution.py:472
  106.9 0.0 copy-start.5
  107.0 0.9 copy.15
  107.9 0.9 copy.14
  108.8 0.0 copy-done.5
  108.8 0.0 copy-start.4
  108.8 1.3 %copy.20 = bf16[256,32,128]{2,1,0:T(8,128)(2,1)} copy(bf16[256,32,128]{2,1,0:T(8,128)(2,1)S(1)} %bitcast.19) | data formatting | bytes 4194304
  110.1 1.0 copy-done.4
  111.2 1.3 %copy.21 = bf16[256,32,128]{2,1,0:T(8,128)(2,1)} copy(bf16[256,32,128]{2,1,0:T(8,128)(2,1)S(1)} %bitcast.18) | data formatting | bytes 4194304
  (1 shorter events, 0.0 us)
Async XLA Ops:
  0.6 1.2 %copy-start.3 = (s32[16,11]{1,0:T(8,128)S(1)}, s32[16,11]{1,0:T(8,128)}, u32[]{:S(2)}) copy-start(s32[16,11]{1,0:T(8,128)} %plan_ref.1) | copy-start | bytes 2116
  0.6 1.2 %copy-start.2 = (s32[16,11]{1,0:T(8,128)S(1)}, s32[16,11]{1,0:T(8,128)}, u32[]{:S(2)}) copy-start(s32[16,11]{1,0:T(8,128)} %block_ref.1) | copy-start | bytes 2116
  0.7 1.2 %copy-start.1 = (s32[16,11]{1,0:T(8,128)S(1)}, s32[16,11]{1,0:T(8,128)}, u32[]{:S(2)}) copy-start(s32[16,11]{1,0:T(8,128)} %length_ref.1) | copy-start | bytes 2116
  0.7 1.2 %copy-start = (f32[16,11]{1,0:T(8,128)S(1)}, f32[16,11]{1,0:T(8,128)}, u32[]{:S(2)}) copy-start(f32[16,11]{1,0:T(8,128)} %reward_ref.1) | copy-start | bytes 2116
  106.9 1.9 %copy-start.5 = (bf16[256,4,8,128]{3,2,1,0:T(8,128)(2,1)S(1)}, bf16[256,4,8,128]{3,2,1,0:T(8,128)(2,1)}, u32[]{:S(2)}) copy-start(bf16[256,4,8,128]{3,2,1,0:T(8,128)(2,1)} %get-tuple-element.7) | copy-start | bytes 6291460
  108.8 2.3 %copy-start.4 = (bf16[256,4,8,128]{3,2,1,0:T(8,128)(2,1)S(1)}, bf16[256,4,8,128]{3,2,1,0:T(8,128)(2,1)}, u32[]{:S(2)}) copy-start(bf16[256,4,8,128]{3,2,1,0:T(8,128)(2,1)} %get-tuple-element.8) | copy-start | bytes 6291460

commit v7 on v6

--- a/solution.py
+++ b/solution.py
@@ -84,6 +84,8 @@
     is_edge = seq == boundary - 1
     is_relay = seq == boundary
     twin = dp + 2 - 4 * lax.rem(dp // 2, 2)
+    late = seq < boundary
+    early = seq >= boundary
     plain_next = has_next & jnp.logical_not(is_edge)
 
     barrier = pltpu.get_barrier_semaphore()
@@ -292,16 +294,21 @@
                     for n, at in enumerate((start_head, end_head)):
                         gather_step(g1, 2 + n, more1 & at)
                         relay_step(g1, 2 + n, more1 & at)
-                    chain_step(b2, 4, done2 & start_head)
+                    chain_step(b2, 4, done2 & start_head & early)
+                    chain_step(0, 2, (g == kv_count - 1) & start_head & late)
                     chain_step(g, 0, end_head)
                 if p == 1:
                     for n, at in enumerate((start_head, end_head)):
                         gather_step(g2, n, more2 & at)
                         relay_step(g2, n, more2 & at)
-                    chain_step(b1, 2, done1 & start_head)
-                    chain_step(b1, 3, done1 & end_head)
+                    chain_step(b1, 2, done1 & start_head & early)
+                    chain_step(b1, 3, done1 & end_head & early)
+                    chain_step(0, 1, (g == kv_count - 2) & end_head & late)
+                    chain_step(0, 3, (g == kv_count - 1) & start_head & late)
+                    chain_step(0, 4, (g == kv_count - 1) & end_head & late)
+                    chain_step(1, 1, (g == kv_count - 1) & end_head & late)
                 if p == 3:
-                    chain_step(g, 1, end_head)
+                    chain_step(g, 1, end_head & early)
 
             @pl.when(start_head)
             def _():
@@ -338,10 +345,22 @@
 
         lax.fori_loop(0, kv_count * here, turn, 0)
         final = kv_count - 1
-        chain_step(final, 2)
-        chain_step(final - 1, 4)
-        chain_step(final, 3)
-        chain_step(final, 4)
+
+        @pl.when(early)
+        def _():
+            chain_step(final, 2)
+            chain_step(final - 1, 4)
+            chain_step(final, 3)
+            chain_step(final, 4)
+
+        @pl.when(late)
+        def _():
+            for total in range(3, final + 5):
+                for g in range(1, kv_count):
+                    k = total - g
+                    if 1 <= k <= 4 and (g, k) != (1, 1):
+                        chain_step(g, k)
+
         for g in range(kv_count):
             for k in range(4):
                 for w in range(2):

time: 113 us -> 100 us (0.88)
  Pallas kernels: 105 us -> 92.5 us
    pallas_call x1, Pallas kernels: 105 us -> 92.5 us  [attention(): pl.pallas_call(functools.partial(kernel, groups, seq_count, short_rows, s...]
where the time goes in v7:
time: 100 us; the launch traced here: 99.9 us
  Pallas kernels  92.5 us (92%)
  local copies, waits for them, and re-layouts  6.66 us (7%)
    pallas_call x1, Pallas kernels, attention(): pl.pallas_call(functools.partial(kernel, groups, seq_count, short_rows, s...  92.5 us
    unnamed x16, local copies, waits for them, and re-layouts  5.5 us

profile of v7, /device:TPU:134, one launch (start us, length us, event | category | flops | bytes accessed | tf_op | source)
XLA Modules:
  0.0 99.9 jit_solution(14765879478144558906)
XLA Ops:
  0.6 0.0 copy-start.3
  0.6 0.0 copy-start.2
  0.7 0.0 copy-start.1
  0.7 0.0 copy-start
  0.7 1.1 %copy_bitcast_fusion = (bf16[1,256,4,128]{3,1,0,2:T(8,128)(2,1)S(1)}, bf16[1,256,4,128]{3,1,0,2:T(8,128)(2,1)S(1)}) fusion(bf16[256,4,128]{2,1,0:T(4,128)(2,1)} %param.10, bf16[256,4,128]{2,1,0:T(4,128)(2,1)} %param.9), kind=kLoop, calls=%fused_computation.3 | loop fusion | bytes 1048576 | tf_op jit(solution)/shard_map/stack | solution.py:534
  1.8 0.1 maximum_bitcast_fusion.kv_hbm
  1.9 0.0 copy-done.3
  1.9 0.0 copy-done.2
  1.9 0.0 copy-done.1
  1.9 0.0 copy-done
  1.9 92.5 %shard_map.111 = (bf16[256,4,8,128]{3,2,1,0:T(8,128)(2,1)}, bf16[256,4,8,128]{3,2,1,0:T(8,128)(2,1)}, bf16[4,2,256,128]{3,2,1,0:T(8,128)(2,1)S(1)}) custom-call(bf16[256,4,8,128]{3,2,1,0:T(8,128)(2,1)} %bitcast.16, bf16[256,4,8,128]{3,2,1,0:T(8,128)(2,1)} %bitcast.17, bf16[4,2,256,128]{3,2,1,0:T(8,128)(2,1)S(1)} %maximum_bitcast_fusion.kv_hbm, ...), custom_call_target="tpu_custom_call" | custom-call | tf_op jit(solution)/shard_map/pallas_call | solution.py:491
  94.4 0.0 copy-start.5
  94.5 0.9 copy.15
  95.4 0.9 copy.14
  96.3 0.0 copy-done.5
  96.3 0.0 copy-start.4
  96.3 1.3 %copy.20 = bf16[256,32,128]{2,1,0:T(8,128)(2,1)} copy(bf16[256,32,128]{2,1,0:T(8,128)(2,1)S(1)} %bitcast.19) | data formatting | bytes 4194304
  97.6 1.0 %copy-done.4 = bf16[256,4,8,128]{3,2,1,0:T(8,128)(2,1)S(1)} copy-done((bf16[256,4,8,128]{3,2,1,0:T(8,128)(2,1)S(1)}, bf16[256,4,8,128]{3,2,1,0:T(8,128)(2,1)}, u32[]{:S(2)}) %copy-start.4) | copy-done | bytes 2097176
  98.6 1.3 %copy.21 = bf16[256,32,128]{2,1,0:T(8,128)(2,1)} copy(bf16[256,32,128]{2,1,0:T(8,128)(2,1)S(1)} %bitcast.18) | data formatting | bytes 4194304
  (1 shorter events, 0.0 us)
Async XLA Ops:
  0.6 1.2 %copy-start.3 = (s32[16,11]{1,0:T(8,128)S(1)}, s32[16,11]{1,0:T(8,128)}, u32[]{:S(2)}) copy-start(s32[16,11]{1,0:T(8,128)} %plan_ref.1) | copy-start | bytes 2116
  0.6 1.2 %copy-start.2 = (s32[16,11]{1,0:T(8,128)S(1)}, s32[16,11]{1,0:T(8,128)}, u32[]{:S(2)}) copy-start(s32[16,11]{1,0:T(8,128)} %block_ref.1) | copy-start | bytes 2116
  0.7 1.2 %copy-start.1 = (s32[16,11]{1,0:T(8,128)S(1)}, s32[16,11]{1,0:T(8,128)}, u32[]{:S(2)}) copy-start(s32[16,11]{1,0:T(8,128)} %length_ref.1) | copy-start | bytes 2116
  0.7 1.2 %copy-start = (f32[16,11]{1,0:T(8,128)S(1)}, f32[16,11]{1,0:T(8,128)}, u32[]{:S(2)}) copy-start(f32[16,11]{1,0:T(8,128)} %reward_ref.1) | copy-start | bytes 2116
  94.4 1.9 %copy-start.5 = (bf16[256,4,8,128]{3,2,1,0:T(8,128)(2,1)S(1)}, bf16[256,4,8,128]{3,2,1,0:T(8,128)(2,1)}, u32[]{:S(2)}) copy-start(bf16[256,4,8,128]{3,2,1,0:T(8,128)(2,1)} %get-tuple-element.7) | copy-start | bytes 6291460
  96.3 2.3 %copy-start.4 = (bf16[256,4,8,128]{3,2,1,0:T(8,128)(2,1)S(1)}, bf16[256,4,8,128]{3,2,1,0:T(8,128)(2,1)}, u32[]{:S(2)}) copy-start(bf16[256,4,8,128]{3,2,1,0:T(8,128)(2,1)} %get-tuple-element.8) | copy-start | bytes 6291460

commit v8 on v7

--- a/solution.py
+++ b/solution.py
@@ -187,7 +187,7 @@
             return hop(relay_v.at[g, w, at], kw.at[g, w, at], relay_send, gather_recv, {"dp": twin, "seq": boundary}, g, k, w)
 
         def gather_arrived(g, k, w, when=True):
-            @pl.when(has_prev & when)
+            @pl.when((seq > short_rows + k) & when)
             def _():
                 gather(g, k, w).wait_recv()
 
@@ -196,7 +196,7 @@
                 if k > 0:
                     gather_arrived(g, k - 1, w, when)
 
-                @pl.when(plain_next & when)
+                @pl.when(plain_next & (seq >= short_rows + k) & when)
                 def _():
                     gather(g, k, w).start()
 
@@ -227,7 +227,7 @@
         def chain_step(g, k, when=True):
             for w in range(2):
                 if k > 0:
-                    @pl.when(has_next & when)
+                    @pl.when(has_next & (seq >= short_rows + 4 - k) & when)
                     def _():
                         chain(g, k - 1, w).wait_recv()
                         got = part_rows[k - 1]
@@ -235,7 +235,7 @@
                         dkv[g, w, at] += rbuf[g, k - 1, w, :got].astype(jnp.float32)
 
                 if k < 4:
-                    @pl.when(has_prev & when)
+                    @pl.when(has_prev & (seq >= short_rows + 4 - k) & when)
                     def _():
                         sbuf[g, k, w, : part_rows[k]] = dkv[g, w, pl.ds(part_at[k], part_rows[k])].astype(jnp.bfloat16)
                         chain(g, k, w).start()
@@ -249,9 +249,11 @@
                             dkv_ref[g, 1] = total.astype(jnp.bfloat16)
 
         def clear_first():
-            @pl.when(jnp.logical_not(has_prev))
-            def _():
-                kw[:, :, :OWN] = jnp.zeros((kv_count, 2, OWN, DH), kw.dtype)
+            for n in range(4):
+                @pl.when(seq == short_rows + n)
+                def _():
+                    empty = OWN - n * tokens
+                    kw[:, :, :empty] = jnp.zeros((kv_count, 2, empty, DH), kw.dtype)
 
         gather_step(0, 0)
         clear_first()
@@ -364,7 +366,7 @@
         for g in range(kv_count):
             for k in range(4):
                 for w in range(2):
-                    @pl.when(has_next)
+                    @pl.when(has_next & (seq >= short_rows + k))
                     def _():
                         gather(g, k, w).wait_send()
 
@@ -372,7 +374,7 @@
                     def _():
                         relay(g, k, w).wait_send()
 
-                    @pl.when(has_prev)
+                    @pl.when(has_prev & (seq >= short_rows + 4 - k))
                     def _():
                         chain(g, k, w).wait_send()
 

time: 100 us -> 97.1 us (0.971)
  Pallas kernels: 92.5 us -> 89.2 us
    pallas_call x1, Pallas kernels: 92.5 us -> 89.2 us  [attention(): pl.pallas_call(functools.partial(kernel, groups, seq_count, short_rows, s...]
where the time goes in v8:
time: 97.1 us; the launch traced here: 96.6 us
  Pallas kernels  89.2 us (92%)
  local copies, waits for them, and re-layouts  6.66 us (7%)
    pallas_call x1, Pallas kernels, attention(): pl.pallas_call(functools.partial(kernel, groups, seq_count, short_rows, s...  89.2 us
    unnamed x16, local copies, waits for them, and re-layouts  5.5 us

profile of v8, /device:TPU:134, one launch (start us, length us, event | category | flops | bytes accessed | tf_op | source)
XLA Modules:
  0.0 96.6 jit_solution(2422509800989120216)
XLA Ops:
  0.6 0.0 copy-start.3
  0.6 0.0 copy-start.2
  0.7 0.0 copy-start.1
  0.7 0.0 copy-start
  0.7 1.1 %copy_bitcast_fusion = (bf16[1,256,4,128]{3,1,0,2:T(8,128)(2,1)S(1)}, bf16[1,256,4,128]{3,1,0,2:T(8,128)(2,1)S(1)}) fusion(bf16[256,4,128]{2,1,0:T(4,128)(2,1)} %param.10, bf16[256,4,128]{2,1,0:T(4,128)(2,1)} %param.9), kind=kLoop, calls=%fused_computation.3 | loop fusion | bytes 1048576 | tf_op jit(solution)/shard_map/stack | solution.py:536
  1.8 0.1 maximum_bitcast_fusion.kv_hbm
  1.9 0.0 copy-done.3
  1.9 0.0 copy-done.2
  1.9 0.0 copy-done.1
  1.9 0.0 copy-done
  1.9 89.2 %shard_map.111 = (bf16[256,4,8,128]{3,2,1,0:T(8,128)(2,1)}, bf16[256,4,8,128]{3,2,1,0:T(8,128)(2,1)}, bf16[4,2,256,128]{3,2,1,0:T(8,128)(2,1)S(1)}) custom-call(bf16[256,4,8,128]{3,2,1,0:T(8,128)(2,1)} %bitcast.16, bf16[256,4,8,128]{3,2,1,0:T(8,128)(2,1)} %bitcast.17, bf16[4,2,256,128]{3,2,1,0:T(8,128)(2,1)S(1)} %maximum_bitcast_fusion.kv_hbm, ...), custom_call_target="tpu_custom_call" | custom-call | tf_op jit(solution)/shard_map/pallas_call | solution.py:493
  91.1 0.0 copy-start.5
  91.1 0.9 copy.15
  92.0 0.9 copy.14
  92.9 0.0 copy-done.5
  92.9 0.0 copy-start.4
  92.9 1.3 %copy.20 = bf16[256,32,128]{2,1,0:T(8,128)(2,1)} copy(bf16[256,32,128]{2,1,0:T(8,128)(2,1)S(1)} %bitcast.19) | data formatting | bytes 4194304
  94.3 1.0 %copy-done.4 = bf16[256,4,8,128]{3,2,1,0:T(8,128)(2,1)S(1)} copy-done((bf16[256,4,8,128]{3,2,1,0:T(8,128)(2,1)S(1)}, bf16[256,4,8,128]{3,2,1,0:T(8,128)(2,1)}, u32[]{:S(2)}) %copy-start.4) | copy-done | bytes 2097176
  95.3 1.3 %copy.21 = bf16[256,32,128]{2,1,0:T(8,128)(2,1)} copy(bf16[256,32,128]{2,1,0:T(8,128)(2,1)S(1)} %bitcast.18) | data formatting | bytes 4194304
  (1 shorter events, 0.0 us)
Async XLA Ops:
  0.6 1.2 %copy-start.3 = (s32[16,11]{1,0:T(8,128)S(1)}, s32[16,11]{1,0:T(8,128)}, u32[]{:S(2)}) copy-start(s32[16,11]{1,0:T(8,128)} %plan_ref.1) | copy-start | bytes 2116
  0.6 1.2 %copy-start.2 = (s32[16,11]{1,0:T(8,128)S(1)}, s32[16,11]{1,0:T(8,128)}, u32[]{:S(2)}) copy-start(s32[16,11]{1,0:T(8,128)} %block_ref.1) | copy-start | bytes 2116
  0.7 1.2 %copy-start.1 = (s32[16,11]{1,0:T(8,128)S(1)}, s32[16,11]{1,0:T(8,128)}, u32[]{:S(2)}) copy-start(s32[16,11]{1,0:T(8,128)} %length_ref.1) | copy-start | bytes 2116
  0.7 1.2 %copy-start = (f32[16,11]{1,0:T(8,128)S(1)}, f32[16,11]{1,0:T(8,128)}, u32[]{:S(2)}) copy-start(f32[16,11]{1,0:T(8,128)} %reward_ref.1) | copy-start | bytes 2116
  91.1 1.9 %copy-start.5 = (bf16[256,4,8,128]{3,2,1,0:T(8,128)(2,1)S(1)}, bf16[256,4,8,128]{3,2,1,0:T(8,128)(2,1)}, u32[]{:S(2)}) copy-start(bf16[256,4,8,128]{3,2,1,0:T(8,128)(2,1)} %get-tuple-element.7) | copy-start | bytes 6291460
  92.9 2.3 %copy-start.4 = (bf16[256,4,8,128]{3,2,1,0:T(8,128)(2,1)S(1)}, bf16[256,4,8,128]{3,2,1,0:T(8,128)(2,1)}, u32[]{:S(2)}) copy-start(bf16[256,4,8,128]{3,2,1,0:T(8,128)(2,1)} %get-tuple-element.8) | copy-start | bytes 6291460

commit v9 on v8

--- a/solution.py
+++ b/solution.py
@@ -67,8 +67,8 @@
 
 
 def kernel(groups, seq_count, short_rows, boundary, q_hbm, up_hbm, kv_hbm, reward_ref, length_ref, block_ref, plan_ref,
-           o_ref, dq_ref, dkv_ref,
-           q_v, up_v, kw, relay_v, kt, dkv, s_ref, p_ref, sbuf, rbuf,
+           o_hbm, dq_hbm, dkv_ref,
+           o_ref, dq_ref, q_v, up_v, kw, relay_v, kt, dkv, s_ref, p_ref, sbuf, rbuf,
            r1q0, r1q1, s2q0, s2q1, r1k0, r1k1, s2k0, s2k1, source_ref,
            load_sem, gather_send, gather_recv, relay_send, relay_recv, chain_send, chain_recv, x_send, x_recv):
     seq = lax.axis_index("seq")
@@ -155,6 +155,8 @@
         )
         o_ref[spot, g] = out.reshape(BLK, per, DH).astype(jnp.bfloat16)
         dq_ref[spot, g] = dq.reshape(BLK, per, DH).astype(jnp.bfloat16)
+        pltpu.make_async_copy(o_ref.at[spot, g], o_hbm.at[spot, g], load_sem.at[3]).start()
+        pltpu.make_async_copy(dq_ref.at[spot, g], dq_hbm.at[spot, g], load_sem.at[4]).start()
 
     up_load = pltpu.make_async_copy(up_hbm, up_v, load_sem.at[0])
 
@@ -264,12 +266,12 @@
         gather_step(0, 1)
         relay_step(0, 1)
         gather_step(0, 2)
+        relay_step(0, 2)
         gather_step(1, 0)
-        relay_step(0, 2)
         relay_step(1, 0)
+        relay_step(0, 3)
         gather_step(0, 3)
         gather_step(1, 1)
-        relay_step(0, 3)
         relay_step(1, 1)
 
         mean = row_mean(dp)
@@ -294,15 +296,15 @@
             def hook(p):
                 if p == 0:
                     for n, at in enumerate((start_head, end_head)):
+                        relay_step(g1, 2 + n, more1 & at)
                         gather_step(g1, 2 + n, more1 & at)
-                        relay_step(g1, 2 + n, more1 & at)
                     chain_step(b2, 4, done2 & start_head & early)
                     chain_step(0, 2, (g == kv_count - 1) & start_head & late)
                     chain_step(g, 0, end_head)
                 if p == 1:
                     for n, at in enumerate((start_head, end_head)):
+                        relay_step(g2, n, more2 & at)
                         gather_step(g2, n, more2 & at)
-                        relay_step(g2, n, more2 & at)
                     chain_step(b1, 2, done1 & start_head & early)
                     chain_step(b1, 3, done1 & end_head & early)
                     chain_step(0, 1, (g == kv_count - 2) & end_head & late)
@@ -475,6 +477,9 @@
             for phase in range(2):
                 pltpu.make_async_copy(s2q[i].at[most], s2q[i].at[most], x_send.at[4 * i + 2 * phase]).wait()
                 pltpu.make_async_copy(s2k[i].at[most], s2k[i].at[most], x_send.at[4 * i + 2 * phase + 1]).wait()
+
+    pltpu.make_async_copy(o_ref, o_hbm, load_sem.at[3]).wait()
+    pltpu.make_async_copy(dq_ref, dq_hbm, load_sem.at[4]).wait()
 
 
 def attention(q, up, kv, plans, groups, seq_count, short_rows):
@@ -493,13 +498,15 @@
     return pl.pallas_call(
         functools.partial(kernel, groups, seq_count, short_rows, seq_count // 2),
         in_specs=[any_spec, any_spec, any_spec, smem, smem, smem, smem],
-        out_specs=[vmem, vmem, vmem],
+        out_specs=[any_spec, any_spec, vmem],
         out_shape=[
             jax.ShapeDtypeStruct(q.shape, half),
             jax.ShapeDtypeStruct(q.shape, half),
             jax.ShapeDtypeStruct(kv.shape, half),
         ],
         scratch_shapes=[
+            pltpu.VMEM(q.shape, half),
+            pltpu.VMEM(q.shape, half),
             pltpu.VMEM(q.shape, half),
             pltpu.VMEM(q.shape, half),
             pltpu.VMEM((kv_count, 2, WINDOW, DH), half),
@@ -513,7 +520,7 @@
             q_pieces, q_pieces, q_pieces, q_pieces,
             kv_pieces, kv_pieces, kv_pieces, kv_pieces,
             pltpu.SMEM((tokens // BLK, groups), jnp.int32),
-            pltpu.SemaphoreType.DMA((3,)),
+            pltpu.SemaphoreType.DMA((5,)),
             per_hop, per_hop, per_hop, per_hop, per_hop, per_hop,
             pltpu.SemaphoreType.DMA((8,)),
             pltpu.SemaphoreType.DMA((8,)),

time: 97.1 us -> 93.9 us (0.967); the launches traced: 96.6 us -> 92.2 us
  Pallas kernels: 89.2 us -> 84.7 us
    pallas_call x1, Pallas kernels: 89.2 us -> 84.7 us  [attention(): pl.pallas_call(functools.partial(kernel, groups, seq_count, short_rows, s...]
where the time goes in v9:
time: 93.9 us; the launch traced here: 92.2 us
  Pallas kernels  84.7 us (90%)
  local copies, waits for them, and re-layouts  6.66 us (7%)
    pallas_call x1, Pallas kernels, attention(): pl.pallas_call(functools.partial(kernel, groups, seq_count, short_rows, s...  84.7 us
    unnamed x16, local copies, waits for them, and re-layouts  5.5 us

profile of v9, /device:TPU:134, one launch (start us, length us, event | category | flops | bytes accessed | tf_op | source)
XLA Modules:
  0.0 92.2 jit_solution(9000294675461310098)
XLA Ops:
  0.6 0.0 copy-start.3
  0.6 0.0 copy-start.2
  0.7 0.0 copy-start.1
  0.7 0.0 copy-start
  0.7 1.1 %copy_bitcast_fusion = (bf16[1,256,4,128]{3,1,0,2:T(8,128)(2,1)S(1)}, bf16[1,256,4,128]{3,1,0,2:T(8,128)(2,1)S(1)}) fusion(bf16[256,4,128]{2,1,0:T(4,128)(2,1)} %param.10, bf16[256,4,128]{2,1,0:T(4,128)(2,1)} %param.9), kind=kLoop, calls=%fused_computation.3 | loop fusion | bytes 1048576 | tf_op jit(solution)/shard_map/stack | solution.py:543
  1.8 0.1 maximum_bitcast_fusion.kv_hbm
  1.9 0.0 copy-done.3
  1.9 0.0 copy-done.2
  1.9 0.0 copy-done.1
  1.9 0.0 copy-done
  1.9 84.7 %shard_map.111 = (bf16[256,4,8,128]{3,2,1,0:T(8,128)(2,1)}, bf16[256,4,8,128]{3,2,1,0:T(8,128)(2,1)}, bf16[4,2,256,128]{3,2,1,0:T(8,128)(2,1)S(1)}) custom-call(bf16[256,4,8,128]{3,2,1,0:T(8,128)(2,1)} %bitcast.16, bf16[256,4,8,128]{3,2,1,0:T(8,128)(2,1)} %bitcast.17, bf16[4,2,256,128]{3,2,1,0:T(8,128)(2,1)S(1)} %maximum_bitcast_fusion.kv_hbm, ...), custom_call_target="tpu_custom_call" | custom-call | tf_op jit(solution)/shard_map/pallas_call | solution.py:498
  86.6 0.0 copy-start.5
  86.7 0.9 copy.15
  87.6 0.9 copy.14
  88.5 0.0 copy-done.5
  88.5 0.0 copy-start.4
  88.5 1.3 %copy.20 = bf16[256,32,128]{2,1,0:T(8,128)(2,1)} copy(bf16[256,32,128]{2,1,0:T(8,128)(2,1)S(1)} %bitcast.19) | data formatting | bytes 4194304
  89.8 1.0 %copy-done.4 = bf16[256,4,8,128]{3,2,1,0:T(8,128)(2,1)S(1)} copy-done((bf16[256,4,8,128]{3,2,1,0:T(8,128)(2,1)S(1)}, bf16[256,4,8,128]{3,2,1,0:T(8,128)(2,1)}, u32[]{:S(2)}) %copy-start.4) | copy-done | bytes 2097176
  90.8 1.3 %copy.21 = bf16[256,32,128]{2,1,0:T(8,128)(2,1)} copy(bf16[256,32,128]{2,1,0:T(8,128)(2,1)S(1)} %bitcast.18) | data formatting | bytes 4194304
  (1 shorter events, 0.0 us)
Async XLA Ops:
  0.6 1.2 %copy-start.3 = (s32[16,11]{1,0:T(8,128)S(1)}, s32[16,11]{1,0:T(8,128)}, u32[]{:S(2)}) copy-start(s32[16,11]{1,0:T(8,128)} %plan_ref.1) | copy-start | bytes 2116
  0.6 1.2 %copy-start.2 = (s32[16,11]{1,0:T(8,128)S(1)}, s32[16,11]{1,0:T(8,128)}, u32[]{:S(2)}) copy-start(s32[16,11]{1,0:T(8,128)} %block_ref.1) | copy-start | bytes 2116
  0.7 1.2 %copy-start.1 = (s32[16,11]{1,0:T(8,128)S(1)}, s32[16,11]{1,0:T(8,128)}, u32[]{:S(2)}) copy-start(s32[16,11]{1,0:T(8,128)} %length_ref.1) | copy-start | bytes 2116
  0.7 1.2 %copy-start = (f32[16,11]{1,0:T(8,128)S(1)}, f32[16,11]{1,0:T(8,128)}, u32[]{:S(2)}) copy-start(f32[16,11]{1,0:T(8,128)} %reward_ref.1) | copy-start | bytes 2116
  86.6 1.9 %copy-start.5 = (bf16[256,4,8,128]{3,2,1,0:T(8,128)(2,1)S(1)}, bf16[256,4,8,128]{3,2,1,0:T(8,128)(2,1)}, u32[]{:S(2)}) copy-start(bf16[256,4,8,128]{3,2,1,0:T(8,128)(2,1)} %get-tuple-element.7) | copy-start | bytes 6291460
  88.5 2.3 %copy-start.4 = (bf16[256,4,8,128]{3,2,1,0:T(8,128)(2,1)S(1)}, bf16[256,4,8,128]{3,2,1,0:T(8,128)(2,1)}, u32[]{:S(2)}) copy-start(bf16[256,4,8,128]{3,2,1,0:T(8,128)(2,1)} %get-tuple-element.8) | copy-start | bytes 6291460

commit v10 on v9

--- a/solution.py
+++ b/solution.py
@@ -165,7 +165,6 @@
         q_load = pltpu.make_async_copy(q_hbm, q_v, load_sem.at[1])
         kv_load = pltpu.make_async_copy(kv_hbm, kw.at[:, :, pl.ds(OWN, tokens)], load_sem.at[2])
         kv_load.start()
-        kv_load.wait()
         hop_from = (OWN, OWN - tokens, OWN - 2 * tokens, BLK * 2)
         hop_to = (OWN - tokens, OWN - 2 * tokens, OWN - 3 * tokens, 0)
         hop_rows = (tokens, tokens, tokens, BLK)
@@ -176,12 +175,15 @@
                 device_id=device, device_id_type=MESH,
             )
 
+        def outgoing(g, k, w):
+            return kv_hbm.at[g, w] if k == 0 else kw.at[g, w, pl.ds(hop_from[k], hop_rows[k])]
+
         def gather(g, k, w):
-            return hop(kw.at[g, w, pl.ds(hop_from[k], hop_rows[k])], kw.at[g, w, pl.ds(hop_to[k], hop_rows[k])],
+            return hop(outgoing(g, k, w), kw.at[g, w, pl.ds(hop_to[k], hop_rows[k])],
                        gather_send, gather_recv, {"seq": seq + 1}, g, k, w)
 
         def edge(g, k, w):
-            return hop(kw.at[g, w, pl.ds(hop_from[k], hop_rows[k])], relay_v.at[g, w, pl.ds(hop_to[k], hop_rows[k])],
+            return hop(outgoing(g, k, w), relay_v.at[g, w, pl.ds(hop_to[k], hop_rows[k])],
                        gather_send, relay_recv, {"dp": twin, "seq": boundary}, g, k, w)
 
         def relay(g, k, w):
@@ -280,6 +282,7 @@
         gain = [reward_ref[dp, j] - mean for j in range(SHORTS, rolls)]
         base = seq * tokens - OWN
 
+        kv_load.wait()
         q_load.wait()
         up_load.wait()
         gather_arrived(0, 3, 0)

time: 93.9 us -> 93.9 us (level)
  no operation moved by 1% of the time
where the time goes in v10:
time: 93.9 us; the launch traced here: 92.3 us
  Pallas kernels  84.9 us (90%)
  local copies, waits for them, and re-layouts  6.66 us (7%)
    pallas_call x1, Pallas kernels, attention(): pl.pallas_call(functools.partial(kernel, groups, seq_count, short_rows, s...  84.9 us
    unnamed x16, local copies, waits for them, and re-layouts  5.5 us

profile of v10, /device:TPU:134, one launch (start us, length us, event | category | flops | bytes accessed | tf_op | source)
XLA Modules:
  0.0 92.3 jit_solution(18236610872754407237)
XLA Ops:
  0.6 0.0 copy-start.3
  0.6 0.0 copy-start.2
  0.7 0.0 copy-start.1
  0.7 0.0 copy-start
  0.7 1.1 %copy_bitcast_fusion = (bf16[1,256,4,128]{3,1,0,2:T(8,128)(2,1)S(1)}, bf16[1,256,4,128]{3,1,0,2:T(8,128)(2,1)S(1)}) fusion(bf16[256,4,128]{2,1,0:T(4,128)(2,1)} %param.10, bf16[256,4,128]{2,1,0:T(4,128)(2,1)} %param.9), kind=kLoop, calls=%fused_computation.3 | loop fusion | bytes 1048576 | tf_op jit(solution)/shard_map/stack | solution.py:546
  1.8 0.1 maximum_bitcast_fusion.kv_hbm
  1.9 0.0 copy-done.3
  1.9 0.0 copy-done.2
  1.9 0.0 copy-done.1
  1.9 0.0 copy-done
  1.9 84.9 %shard_map.111 = (bf16[256,4,8,128]{3,2,1,0:T(8,128)(2,1)}, bf16[256,4,8,128]{3,2,1,0:T(8,128)(2,1)}, bf16[4,2,256,128]{3,2,1,0:T(8,128)(2,1)S(1)}) custom-call(bf16[256,4,8,128]{3,2,1,0:T(8,128)(2,1)} %bitcast.16, bf16[256,4,8,128]{3,2,1,0:T(8,128)(2,1)} %bitcast.17, bf16[4,2,256,128]{3,2,1,0:T(8,128)(2,1)S(1)} %maximum_bitcast_fusion.kv_hbm, ...), custom_call_target="tpu_custom_call" | custom-call | tf_op jit(solution)/shard_map/pallas_call | solution.py:501
  86.8 0.0 copy-start.5
  86.8 0.9 copy.15
  87.7 0.9 copy.14
  88.6 0.0 copy-done.5
  88.6 0.0 copy-start.4
  88.6 1.3 %copy.20 = bf16[256,32,128]{2,1,0:T(8,128)(2,1)} copy(bf16[256,32,128]{2,1,0:T(8,128)(2,1)S(1)} %bitcast.19) | data formatting | bytes 4194304
  90.0 1.0 %copy-done.4 = bf16[256,4,8,128]{3,2,1,0:T(8,128)(2,1)S(1)} copy-done((bf16[256,4,8,128]{3,2,1,0:T(8,128)(2,1)S(1)}, bf16[256,4,8,128]{3,2,1,0:T(8,128)(2,1)}, u32[]{:S(2)}) %copy-start.4) | copy-done | bytes 2097176
  91.0 1.3 %copy.21 = bf16[256,32,128]{2,1,0:T(8,128)(2,1)} copy(bf16[256,32,128]{2,1,0:T(8,128)(2,1)S(1)} %bitcast.18) | data formatting | bytes 4194304
  (1 shorter events, 0.0 us)
Async XLA Ops:
  0.6 1.2 %copy-start.3 = (s32[16,11]{1,0:T(8,128)S(1)}, s32[16,11]{1,0:T(8,128)}, u32[]{:S(2)}) copy-start(s32[16,11]{1,0:T(8,128)} %plan_ref.1) | copy-start | bytes 2116
  0.6 1.2 %copy-start.2 = (s32[16,11]{1,0:T(8,128)S(1)}, s32[16,11]{1,0:T(8,128)}, u32[]{:S(2)}) copy-start(s32[16,11]{1,0:T(8,128)} %block_ref.1) | copy-start | bytes 2116
  0.7 1.2 %copy-start.1 = (s32[16,11]{1,0:T(8,128)S(1)}, s32[16,11]{1,0:T(8,128)}, u32[]{:S(2)}) copy-start(s32[16,11]{1,0:T(8,128)} %length_ref.1) | copy-start | bytes 2116
  0.7 1.2 %copy-start = (f32[16,11]{1,0:T(8,128)S(1)}, f32[16,11]{1,0:T(8,128)}, u32[]{:S(2)}) copy-start(f32[16,11]{1,0:T(8,128)} %reward_ref.1) | copy-start | bytes 2116
  86.8 1.9 %copy-start.5 = (bf16[256,4,8,128]{3,2,1,0:T(8,128)(2,1)S(1)}, bf16[256,4,8,128]{3,2,1,0:T(8,128)(2,1)}, u32[]{:S(2)}) copy-start(bf16[256,4,8,128]{3,2,1,0:T(8,128)(2,1)} %get-tuple-element.7) | copy-start | bytes 6291460
  88.6 2.3 %copy-start.4 = (bf16[256,4,8,128]{3,2,1,0:T(8,128)(2,1)S(1)}, bf16[256,4,8,128]{3,2,1,0:T(8,128)(2,1)}, u32[]{:S(2)}) copy-start(bf16[256,4,8,128]{3,2,1,0:T(8,128)(2,1)} %get-tuple-element.8) | copy-start | bytes 6291460
